TPU v7x, 512 devices: a whole 4x8x8 slice. The times are simulated.
512 devices in a mesh: ctx: 128 (over y, z_hi, x, core), tp: 4 (over z_lo).
Axes of the slice: x: 4, y: 8, z: 8 (z_hi: 2, z_lo: 4; z = z_hi * 4 + z_lo), core: 2. Of those that a mesh axis runs over, the one named last changes fastest.
Arguments:
- saved_rows: bfloat16 [16384, 3, 8192], P(('ctx', 'tp')), may hold values from -1.5 to 1.5
- grad_out: bfloat16 [16384, 8192], P('ctx', 'tp'), may hold values from -6 to 6
- conv_out: bfloat16 [16384, 8192], P('ctx', 'tp'), may hold values from -6 to 6
- filters: float32 [16384, 512], P('ctx', 'tp'), may hold values from -0.1875 to 0.1875
Outputs:
- d_saved: bfloat16 [16384, 3, 8192], P(('ctx', 'tp'))
- d_filters: float32 [16384, 512], P('ctx', 'tp')
All inputs are finite; a program needn't handle non-finite values.
Results may differ from a plain program's by a relative error of at most 0.0049.
Values may be sent and summed in bfloat16 or wider, within the bound.
No kernel may reach another device: no remote copies, remote signals or barrier semaphores. Data moves between devices by JAX's collectives and lax.ppermute only.
A program may use at most 128 MiB of HBM per device.

v0:
```python
import jax
import jax.numpy as jnp
from jax import lax
from jax.experimental import pallas as pl
from jax.experimental.pallas import tpu as pltpu
from jax.sharding import PartitionSpec as P

GSIZE = 16
B = 128
F32 = jnp.float32
BF = jnp.bfloat16


def fill_pairs(src, which, dst):
    for half in range(2):
        dst[pl.ds(0, 1024), pl.ds(B * half, B)] = src[:, half, which].reshape(1024, B)


def correlate_kernel(h_ref, x_ref, o_ref, d_ref, f_ref, w_ref):
    fill_pairs(x_ref, 0, d_ref)
    d_ref[pl.ds(1024, 256), :] = jnp.zeros((256, 256), BF)
    row = lax.broadcasted_iota(jnp.int32, (B, B), 0)
    col = lax.broadcasted_iota(jnp.int32, (B, B), 1)
    flip = jnp.where((row + col) % B == 0, 1.0, 0.0).astype(BF)
    f_ref[...] = jnp.dot(h_ref[...], flip, preferred_element_type=F32)
    lower = row >= col

    def build(e, before):
        line = jnp.broadcast_to(f_ref[pl.ds(e, 1), :], (B, B))
        turned = pltpu.roll(line, 0, 1, stride=1, stride_axis=0)
        block = jnp.where(lower, turned, before).astype(BF)
        at = pl.multiple_of(e * B, B)
        w_ref[pl.ds(at, B), pl.ds(0, B)] = block
        w_ref[pl.ds(at + B, B), pl.ds(B, B)] = block
        return turned

    w_ref[pl.ds(0, B), pl.ds(B, B)] = jnp.zeros((B, B), BF)
    lax.fori_loop(0, B, build, jnp.zeros((B, B), F32), unroll=2)
    for tile in range(4):
        def body(k, acc):
            at = pl.multiple_of(64 * k, 64)
            left = jnp.concatenate(
                [d_ref[pl.ds(256 * tile + at + 16 * u, 256), :] for u in range(4)], axis=1
            )
            right = w_ref[pl.ds(pl.multiple_of(1024 * k, 1024), 1024), :]
            return acc + jnp.dot(left, right, preferred_element_type=F32)

        acc = lax.fori_loop(0, 16 - 4 * tile, body, jnp.zeros((256, 256), F32))
        for half in range(2):
            part = acc[:, B * half : B * half + B].astype(BF)
            o_ref[pl.ds(16 * tile, 16), half] = part.reshape(16, 16, B)


def lags_kernel(x_ref, o_ref, d_ref, m_ref, t_ref, qa_ref, qb_ref):
    fill_pairs(x_ref, 0, d_ref)
    d_ref[pl.ds(1024, 256), :] = jnp.zeros((256, 256), BF)
    fill_pairs(x_ref, 1, m_ref)
    row = lax.broadcasted_iota(jnp.int32, (B, B), 0)
    col = lax.broadcasted_iota(jnp.int32, (B, B), 1)
    flip = jnp.where(row + col == B - 1, 1.0, 0.0).astype(BF)
    for half in range(2):
        t_ref[pl.ds(B * half, B), :] = lax.dot_general(
            flip,
            m_ref[:, pl.ds(B * half, B)],
            (((1,), (1,)), ((), ())),
            preferred_element_type=F32,
        ).astype(BF)
    for part in range(4):
        depth = 256 * (4 - part)

        def body(k, carry):
            e = 16 * part + k
            gram = jnp.dot(
                t_ref[:, pl.ds(0, depth)],
                d_ref[pl.ds(pl.multiple_of(16 * e, 16), depth), :],
                preferred_element_type=F32,
            )
            qa_ref[2 * e] = gram[:B, :B] + gram[B:, B:]
            qa_ref[2 * e + 1] = gram[:B, B:]
            qb_ref[e] = gram[B:, :B]
            return carry

        lax.fori_loop(0, 16, body, 0)
    qb_ref[64] = jnp.zeros((B, B), F32)
    qa_ref[128] = jnp.zeros((B, B), F32)
    keep = row + col >= B - 1

    def diagonals(e, carry):
        first = qa_ref[2 * e]
        second = qa_ref[2 * e + 1] + qb_ref[e + 1]
        third = qa_ref[2 * e + 2]
        for u, (here, ahead) in enumerate(((first, second), (second, third))):
            turned = pltpu.roll(jnp.where(keep, here, ahead), 1, 1, stride=1, stride_axis=0)
            o_ref[pl.ds(2 * e + u, 1), :] = jnp.sum(turned, axis=0, keepdims=True)
        return carry

    lax.fori_loop(0, 64, diagonals, 0)


def correlate(taps, signals):
    return pl.pallas_call(
        correlate_kernel,
        out_shape=jax.ShapeDtypeStruct((64, 2, GSIZE, B), BF),
        scratch_shapes=[
            pltpu.VMEM((1280, 256), BF),
            pltpu.VMEM((B, B), F32),
            pltpu.VMEM((129 * B, 256), BF),
        ],
        compiler_params=pltpu.CompilerParams(vmem_limit_bytes=32 << 20),
        cost_estimate=pl.CostEstimate(
            flops=160 * 2 * 256**3, bytes_accessed=3 << 20, transcendentals=0
        ),
    )(taps, signals)


def lags(signals):
    return pl.pallas_call(
        lags_kernel,
        out_shape=jax.ShapeDtypeStruct((B, B), F32),
        scratch_shapes=[
            pltpu.VMEM((1280, 256), BF),
            pltpu.VMEM((1024, 256), BF),
            pltpu.VMEM((256, 1024), BF),
            pltpu.VMEM((129, B, B), F32),
            pltpu.VMEM((65, B, B), F32),
        ],
        compiler_params=pltpu.CompilerParams(vmem_limit_bytes=32 << 20),
        cost_estimate=pl.CostEstimate(
            flops=160 * 2 * 256**3, bytes_accessed=3 << 20, transcendentals=0
        ),
    )(signals)


def swap(x, axis):
    return lax.all_to_all(x, axis, split_axis=0, concat_axis=0, tiled=True)


def per_device(saved_rows, grad_out, conv_out, filters):
    rows, _, width = saved_rows.shape
    tokens, own = grad_out.shape
    parts = width // own
    query, key, value = (saved_rows[:, i, :].astype(F32) for i in range(3))
    mixed_rows = (key * value).astype(BF)
    taps = swap(filters.T.astype(BF), "ctx")
    outward = jnp.stack(
        [x.reshape(rows, parts, own).transpose(1, 0, 2) for x in (saved_rows[:, 0, :], mixed_rows)],
        axis=1,
    )
    arrived = swap(outward, "tp")
    query_cols = arrived[:, 0].reshape(tokens, own).astype(F32)
    mixed = arrived[:, 1].reshape(tokens, own)
    grad_wide = grad_out.astype(F32)
    delta = (query_cols * grad_wide).astype(BF)
    blocks = own // GSIZE
    spread = jnp.stack(
        [delta.T.reshape(blocks, GSIZE, tokens), mixed.T.reshape(blocks, GSIZE, tokens)], axis=1
    )
    signals = swap(spread, "ctx").reshape(blocks // 2, 2, 2, GSIZE, tokens)
    grad_x = correlate(taps, signals).reshape(blocks, GSIZE, tokens)
    back_x = swap(grad_x, "ctx").reshape(own, tokens)
    d_query = (grad_wide * conv_out.astype(F32)).astype(BF)
    grad_h = lags(signals)
    back_h = swap(grad_h, "ctx")
    homeward = jnp.stack(
        [d_query.reshape(parts, rows, own), back_x.T.reshape(parts, rows, own)], axis=1
    )
    home = swap(homeward, "tp")
    d_query_rows, grad_rows = (
        home[:, i].transpose(1, 0, 2).reshape(rows, width) for i in range(2)
    )
    grad_rows = grad_rows.astype(F32)
    d_key = (grad_rows * value).astype(BF)
    d_value = (grad_rows * key).astype(BF)
    return (jnp.stack([d_query_rows, d_key, d_value], axis=1), back_h.T)


def solution(mesh):
    placed = (P(("ctx", "tp"), None, None), P("ctx", "tp"), P("ctx", "tp"), P("ctx", "tp"))
    return jax.shard_map(
        per_device,
        mesh=mesh,
        in_specs=placed,
        out_specs=(P(("ctx", "tp"), None, None), P("ctx", "tp")),
        check_vma=False,
    )
```

profile of v0, /device:TPU:1, one launch (start us, length us, event | category | flops | bytes accessed | tf_op | source)
XLA Modules:
  0.0 227.4 jit_solution(332965808491242550)
XLA Ops:
  0.6 1.4 fusion.3
  2.8 0.7 pad_maximum_fusion.1
  3.6 1.5 copy.45
  5.1 7.8 %all-to-all-start.1 = ((bf16[4,2,32,2048]{3,2,1,0:T(8,128)(2,1)}), bf16[4,2,32,2048]{3,2,1,0:T(8,128)(2,1)S(1)}, u32[]{:S(2)}, u32[]{:S(2)}) async-start(bf16[4,2,32,2048]{3,2,1,0:T(8,128)(2,1)} %copy.45), calls=%async_computation.1 | async-start | bytes 2097152 | tf_op jit(solution)/shard_map/all_to_all | solution.py:135
  13.0 0.7 copy.44
  13.7 24.4 %all-to-all-done.1 = bf16[4,2,32,2048]{3,2,1,0:T(8,128)(2,1)S(1)} async-done(((bf16[4,2,32,2048]{3,2,1,0:T(8,128)(2,1)}), bf16[4,2,32,2048]{3,2,1,0:T(8,128)(2,1)S(1)}, u32[]{:S(2)}, u32[]{:S(2)}) %all-to-all-start.1) | async-done | bytes 1048608 | tf_op jit(solution)/shard_map/all_to_all | solution.py:135
  38.1 18.1 %all-to-all-start = ((bf16[128,1,128]{2,1,0:T(2,128)(2,1)}), bf16[128,1,128]{2,1,0:T(2,128)(2,1)S(1)}, u32[]{:S(2)}, u32[]{:S(2)}) async-start(bf16[128,1,128]{2,1,0:T(2,128)(2,1)} %copy.44), calls=%async_computation | async-start | bytes 131072 | tf_op jit(solution)/shard_map/all_to_all | solution.py:135
  56.7 0.6 copy-done.1
  58.2 1.2 copy.50
  59.3 11.3 %all-to-all-done = bf16[128,1,128]{2,1,0:T(2,128)(2,1)S(1)} async-done(((bf16[128,1,128]{2,1,0:T(2,128)(2,1)}), bf16[128,1,128]{2,1,0:T(2,128)(2,1)S(1)}, u32[]{:S(2)}, u32[]{:S(2)}) %all-to-all-start) | async-done | bytes 32800 | tf_op jit(solution)/shard_map/all_to_all | solution.py:135
  70.7 5.8 %all-to-all-start.2 = ((bf16[128,2,16,128]{3,2,1,0:T(8,128)(2,1)}), bf16[128,2,16,128]{3,2,1,0:T(8,128)(2,1)S(1)}, u32[]{:S(2)}, u32[]{:S(2)}) async-start(bf16[128,2,16,128]{3,2,1,0:T(8,128)(2,1)} %copy.50), calls=%async_computation.2 | async-start | bytes 2097152 | tf_op jit(solution)/shard_map/all_to_all | solution.py:135
  76.6 32.6 %all-to-all-done.2 = bf16[128,2,16,128]{3,2,1,0:T(8,128)(2,1)S(1)} async-done(((bf16[128,2,16,128]{3,2,1,0:T(8,128)(2,1)}), bf16[128,2,16,128]{3,2,1,0:T(8,128)(2,1)S(1)}, u32[]{:S(2)}, u32[]{:S(2)}) %all-to-all-start.2) | async-done | bytes 1048608 | tf_op jit(solution)/shard_map/all_to_all | solution.py:135
  109.1 20.7 %shard_map.59 = bf16[64,2,16,128]{3,2,1,0:T(8,128)(2,1)} custom-call(bf16[128,128]{1,0:T(8,128)(2,1)S(1)} %bitcast.58, bf16[64,2,2,16,128]{4,3,2,1,0:T(8,128)(2,1)S(1)} %bitcast.56), custom_call_target="tpu_custom_call" | custom-call | flops 5368709120 | bytes 3145728 | tf_op jit(solution)/shard_map/pallas_call | solution.py:101
  129.8 7.5 %all-to-all-start.3 = ((bf16[128,16,128]{2,1,0:T(8,128)(2,1)}), bf16[128,16,128]{2,1,0:T(8,128)(2,1)S(1)}, u32[]{:S(2)}, u32[]{:S(2)}) async-start(bf16[128,16,128]{2,1,0:T(8,128)(2,1)} %bitcast.14), calls=%async_computation.3 | async-start | bytes 1048576 | tf_op jit(solution)/shard_map/all_to_all | solution.py:135
  137.3 24.4 %shard_map.60 = f32[128,128]{1,0:T(8,128)} custom-call(bf16[64,2,2,16,128]{4,3,2,1,0:T(8,128)(2,1)S(1)} %bitcast.57), custom_call_target="tpu_custom_call" | custom-call | flops 5368709120 | bytes 3145728 | tf_op jit(solution)/shard_map/pallas_call | solution.py:117
  161.7 16.3 %all-to-all-start.5 = ((f32[128,1,128]{2,1,0:T(1,128)}), f32[128,1,128]{2,1,0:T(1,128)S(1)}, u32[]{:S(2)}, u32[]{:S(2)}) async-start(f32[128,1,128]{2,1,0:T(1,128)} %bitcast.23), calls=%async_computation.5 | async-start | bytes 131072 | tf_op jit(solution)/shard_map/all_to_all | solution.py:135
  178.4 1.0 copy.52
  179.4 13.1 %all-to-all-done.5 = f32[128,1,128]{2,1,0:T(1,128)S(1)} async-done(((f32[128,1,128]{2,1,0:T(1,128)}), f32[128,1,128]{2,1,0:T(1,128)S(1)}, u32[]{:S(2)}, u32[]{:S(2)}) %all-to-all-start.5) | async-done | bytes 65568 | tf_op jit(solution)/shard_map/all_to_all | solution.py:135
  192.5 3.5 %all-to-all-start.4 = ((bf16[4,2,32,2048]{3,2,1,0:T(8,128)(2,1)}), bf16[4,2,32,2048]{3,2,1,0:T(8,128)(2,1)S(1)}, u32[]{:S(2)}, u32[]{:S(2)}) async-start(bf16[4,2,32,2048]{3,2,1,0:T(8,128)(2,1)} %copy.52), calls=%async_computation.4 | async-start | bytes 2097152 | tf_op jit(solution)/shard_map/all_to_all | solution.py:135
  196.0 0.7 copy.56
  196.7 24.5 %all-to-all-done.4 = bf16[4,2,32,2048]{3,2,1,0:T(8,128)(2,1)S(1)} async-done(((bf16[4,2,32,2048]{3,2,1,0:T(8,128)(2,1)}), bf16[4,2,32,2048]{3,2,1,0:T(8,128)(2,1)S(1)}, u32[]{:S(2)}, u32[]{:S(2)}) %all-to-all-start.4) | async-done | bytes 1048608 | tf_op jit(solution)/shard_map/all_to_all | solution.py:135
  222.2 1.6 copy.54
  223.8 2.1 reshape.46
  226.1 1.3 pad_maximum_fusion
  (25 shorter events, 3.6 us)
Async XLA Ops:
  0.6 1.4 slice-start
  3.6 9.4 %copy-start.3 = (f32[128,128]{1,0:T(8,128)S(1)}, f32[128,128]{1,0:T(8,128)}, u32[]{:S(2)}) copy-start(f32[128,128]{1,0:T(8,128)} %param.7) | copy-start | bytes 196612
  5.1 33.0 %all-to-all-start.1 = ((bf16[4,2,32,2048]{3,2,1,0:T(8,128)(2,1)}), bf16[4,2,32,2048]{3,2,1,0:T(8,128)(2,1)S(1)}, u32[]{:S(2)}, u32[]{:S(2)}) async-start(bf16[4,2,32,2048]{3,2,1,0:T(8,128)(2,1)} %copy.45), calls=%async_computation.1 | async-start | bytes 2097152 | tf_op jit(solution)/shard_map/all_to_all | solution.py:135
  38.1 32.5 %all-to-all-start = ((bf16[128,1,128]{2,1,0:T(2,128)(2,1)}), bf16[128,1,128]{2,1,0:T(2,128)(2,1)S(1)}, u32[]{:S(2)}, u32[]{:S(2)}) async-start(bf16[128,1,128]{2,1,0:T(2,128)(2,1)} %copy.44), calls=%async_computation | async-start | bytes 131072 | tf_op jit(solution)/shard_map/all_to_all | solution.py:135
  56.3 1.0 copy-start.1
  56.3 1.2 copy-start.2
  70.7 38.4 %all-to-all-start.2 = ((bf16[128,2,16,128]{3,2,1,0:T(8,128)(2,1)}), bf16[128,2,16,128]{3,2,1,0:T(8,128)(2,1)S(1)}, u32[]{:S(2)}, u32[]{:S(2)}) async-start(bf16[128,2,16,128]{3,2,1,0:T(8,128)(2,1)} %copy.50), calls=%async_computation.2 | async-start | bytes 2097152 | tf_op jit(solution)/shard_map/all_to_all | solution.py:135
  129.8 31.9 %all-to-all-start.3 = ((bf16[128,16,128]{2,1,0:T(8,128)(2,1)}), bf16[128,16,128]{2,1,0:T(8,128)(2,1)S(1)}, u32[]{:S(2)}, u32[]{:S(2)}) async-start(bf16[128,16,128]{2,1,0:T(8,128)(2,1)} %bitcast.14), calls=%async_computation.3 | async-start | bytes 1048576 | tf_op jit(solution)/shard_map/all_to_all | solution.py:135
  161.7 30.8 %all-to-all-start.5 = ((f32[128,1,128]{2,1,0:T(1,128)}), f32[128,1,128]{2,1,0:T(1,128)S(1)}, u32[]{:S(2)}, u32[]{:S(2)}) async-start(f32[128,1,128]{2,1,0:T(1,128)} %bitcast.23), calls=%async_computation.5 | async-start | bytes 131072 | tf_op jit(solution)/shard_map/all_to_all | solution.py:135
  192.5 28.8 %all-to-all-start.4 = ((bf16[4,2,32,2048]{3,2,1,0:T(8,128)(2,1)}), bf16[4,2,32,2048]{3,2,1,0:T(8,128)(2,1)S(1)}, u32[]{:S(2)}, u32[]{:S(2)}) async-start(bf16[4,2,32,2048]{3,2,1,0:T(8,128)(2,1)} %copy.52), calls=%async_computation.4 | async-start | bytes 2097152 | tf_op jit(solution)/shard_map/all_to_all | solution.py:135
  223.8 2.1 copy-start
where the time goes:
time: 228 us; the launch traced here: 227 us
  waiting for transfers between devices  106 us (46%)
  starting transfers between devices  59.1 us (26%)
  Pallas kernels  45 us (20%)
  local copies, waits for them, and re-layouts  12.2 us (5%)
  other arithmetic  4.3 us (2%)
    all_to_all x6, waiting for transfers between devices, swap(): return lax.all_to_all(x, axis, split_axis=0, concat_axis=0, tiled=True)  106 us
    all_to_all x6, starting transfers between devices, swap(): return lax.all_to_all(x, axis, split_axis=0, concat_axis=0, tiled=True)  59.1 us
    pallas_call x1, Pallas kernels, lags(): pl.pallas_call(lags_kernel, out_shape=jax.ShapeDtypeStruct((B, B), F32),...  24.4 us
    pallas_call x1, Pallas kernels, correlate(): pl.pallas_call(correlate_kernel, out_shape=jax.ShapeDtypeStruct((64, 2, G...  20.7 us
  transfers between devices with their start and end apart: 6, of which 5 were waited for; matrix products, arithmetic and copies ran while one was open for 2% of the time, Pallas kernels for 11%

commit v1 on v0

v1 whole, which is shorter than its diff:
```python
import jax
import jax.numpy as jnp
from jax import lax
from jax.experimental import pallas as pl
from jax.experimental.pallas import tpu as pltpu
from jax.sharding import PartitionSpec as P

GSIZE = 16
B = 128
OUT_ROWS = 40
BACK_ROWS = 24
F32 = jnp.float32
BF = jnp.bfloat16


def pack_rows_kernel(s_ref, o_ref):
    o_ref[0, 0] = s_ref[0]
    o_ref[0, 1] = (s_ref[1].astype(F32) * s_ref[2].astype(F32)).astype(BF)


def pack_rows(saved, parts):
    _, rows, width = saved.shape
    own = width // parts
    return pl.pallas_call(
        pack_rows_kernel,
        grid=(parts,),
        in_specs=[pl.BlockSpec((3, rows, own), lambda t: (0, 0, t))],
        out_specs=pl.BlockSpec((1, 2, rows, own), lambda t: (t, 0, 0, 0)),
        out_shape=jax.ShapeDtypeStruct((parts, 2, rows, own), BF),
    )(saved)


def pack_groups_kernel(a_ref, g_ref, c_ref, h_ref, o_ref, q_ref):
    tokens, span = g_ref.shape
    count = span // GSIZE
    grad = g_ref[...].astype(F32)
    q_ref[...] = (grad * c_ref[...].astype(F32)).astype(BF)
    query = a_ref[:, 0].reshape(tokens, span).astype(F32)
    delta = (query * grad).astype(BF)
    o_ref[:, pl.ds(0, GSIZE), :] = delta.T.reshape(count, GSIZE, tokens)
    mixed = a_ref[:, 1].reshape(tokens, span)
    o_ref[:, pl.ds(GSIZE, GSIZE), :] = mixed.T.reshape(count, GSIZE, tokens)
    taps = h_ref[...].T
    o_ref[:, pl.ds(2 * GSIZE, 8), :] = jnp.broadcast_to(
        taps[:, None, :], (count, 8, tokens)
    ).astype(BF)


def pack_groups(arrived, grad_out, conv_out, filters):
    parts, _, rows, own = arrived.shape
    tokens = parts * rows
    groups = own // GSIZE
    return pl.pallas_call(
        pack_groups_kernel,
        in_specs=[pl.BlockSpec(memory_space=pltpu.VMEM)] * 4,
        out_specs=[pl.BlockSpec(memory_space=pltpu.VMEM)] * 2,
        out_shape=(
            jax.ShapeDtypeStruct((groups, OUT_ROWS, tokens), BF),
            jax.ShapeDtypeStruct((tokens, own), BF),
        ),
        compiler_params=pltpu.CompilerParams(vmem_limit_bytes=32 << 20),
    )(arrived, grad_out, conv_out, filters)


def correlate_kernel(x_ref, o_ref, d_ref, m_ref, t_ref, f_ref, w_ref, qa_ref, qb_ref, l_ref):
    for half in range(2):
        lanes = pl.ds(B * half, B)
        d_ref[pl.ds(0, 1024), lanes] = x_ref[:, half, :GSIZE].reshape(1024, B)
        m_ref[:, lanes] = x_ref[:, half, GSIZE : 2 * GSIZE].reshape(1024, B)
    d_ref[pl.ds(1024, 256), :] = jnp.zeros((256, 256), BF)
    row = lax.broadcasted_iota(jnp.int32, (B, B), 0)
    col = lax.broadcasted_iota(jnp.int32, (B, B), 1)

    flip = jnp.where((row + col) % B == 0, 1.0, 0.0).astype(BF)
    taps = x_ref[:, :, 2 * GSIZE :].astype(F32).reshape(1024, B).astype(BF)
    f_ref[...] = jnp.dot(taps, flip, preferred_element_type=F32).reshape(B, 8, B)
    lower = row >= col
    w_ref[pl.ds(0, B), pl.ds(B, B)] = jnp.zeros((B, B), BF)

    def build(e, before):
        line = jnp.broadcast_to(f_ref[pl.ds(e, 1)], (16, 8, B)).reshape(B, B)
        turned = pltpu.roll(line, 0, 1, stride=1, stride_axis=0)
        block = jnp.where(lower, turned, before).astype(BF)
        at = pl.multiple_of(e * B, B)
        w_ref[pl.ds(at, B), pl.ds(0, B)] = block
        w_ref[pl.ds(at + B, B), pl.ds(B, B)] = block
        return turned

    lax.fori_loop(0, B, build, jnp.zeros((B, B), F32), unroll=16)
    for tile in range(4):
        count = 64 - 16 * tile
        left = jnp.concatenate(
            [d_ref[pl.ds(256 * tile + 16 * u, 256), :] for u in range(count)], axis=1
        )
        total = jnp.dot(left, w_ref[pl.ds(0, 256 * count), :], preferred_element_type=F32)
        for half in range(2):
            part = total[:, B * half : B * half + B].astype(BF)
            o_ref[pl.ds(16 * tile, 16), half, pl.ds(0, GSIZE)] = part.reshape(16, GSIZE, B)

    mirror = jnp.where(row + col == B - 1, 1.0, 0.0).astype(BF)
    for half in range(2):
        t_ref[pl.ds(B * half, B), :] = lax.dot_general(
            mirror,
            m_ref[:, pl.ds(B * half, B)],
            (((1,), (1,)), ((), ())),
            preferred_element_type=F32,
        ).astype(BF)
    for part in range(4):
        depth = 256 * (4 - part)

        def gram(k, carry):
            e = 16 * part + k
            table = jnp.dot(
                t_ref[:, pl.ds(0, depth)],
                d_ref[pl.ds(pl.multiple_of(16 * e, 16), depth), :],
                preferred_element_type=F32,
            )
            qa_ref[2 * e] = table[:B, :B] + table[B:, B:]
            qa_ref[2 * e + 1] = table[:B, B:]
            qb_ref[e] = table[B:, :B]
            return carry

        lax.fori_loop(0, 16, gram, 0, unroll=16)
    qb_ref[64] = jnp.zeros((B, B), F32)
    qa_ref[128] = jnp.zeros((B, B), F32)
    keep = row + col >= B - 1

    def diagonals(e, carry):
        first = qa_ref[2 * e]
        second = qa_ref[2 * e + 1] + qb_ref[e + 1]
        third = qa_ref[2 * e + 2]
        for u, (here, ahead) in enumerate(((first, second), (second, third))):
            turned = pltpu.roll(jnp.where(keep, here, ahead), 1, 1, stride=1, stride_axis=0)
            l_ref[pl.ds(2 * e + u, 1), :] = jnp.sum(turned, axis=0, keepdims=True)
        return carry

    lax.fori_loop(0, 64, diagonals, 0, unroll=16)
    sums = l_ref[...]
    coarse = sums.astype(BF).astype(F32)
    fine = sums - coarse
    shape = (B, 8, B)
    pick = lax.broadcasted_iota(jnp.int32, shape, 1) == 0
    both = jnp.where(
        pick, jnp.broadcast_to(coarse[:, None], shape), jnp.broadcast_to(fine[:, None], shape)
    )
    o_ref[:, :, pl.ds(GSIZE, 8)] = both.astype(BF).reshape(64, 2, 8, B)


def correlate(signals):
    return pl.pallas_call(
        correlate_kernel,
        in_specs=[pl.BlockSpec(memory_space=pltpu.VMEM)],
        out_specs=pl.BlockSpec(memory_space=pltpu.VMEM),
        out_shape=jax.ShapeDtypeStruct((64, 2, BACK_ROWS, B), BF),
        scratch_shapes=[
            pltpu.VMEM((1280, 256), BF),
            pltpu.VMEM((1024, 256), BF),
            pltpu.VMEM((256, 1024), BF),
            pltpu.VMEM((B, 8, B), F32),
            pltpu.VMEM((129 * B, 256), BF),
            pltpu.VMEM((129, B, B), F32),
            pltpu.VMEM((65, B, B), F32),
            pltpu.VMEM((B, B), F32),
        ],
        compiler_params=pltpu.CompilerParams(vmem_limit_bytes=40 << 20),
        cost_estimate=pl.CostEstimate(
            flops=640 * 2 * 256**3, bytes_accessed=64 << 20, transcendentals=0
        ),
    )(signals)


def unpack_groups_kernel(b_ref, x_ref, h_ref):
    groups = b_ref.shape[0]
    tokens = b_ref.shape[2]
    x_ref[...] = b_ref[:, :GSIZE].reshape(groups * GSIZE, tokens).T
    tail = b_ref[:, GSIZE:].astype(F32)
    row = lax.broadcasted_iota(jnp.int32, tail.shape, 1)
    h_ref[...] = jnp.sum(jnp.where(row < 2, tail, 0.0), axis=1).T


def unpack_groups(back):
    groups, _, tokens = back.shape
    return pl.pallas_call(
        unpack_groups_kernel,
        in_specs=[pl.BlockSpec(memory_space=pltpu.VMEM)],
        out_specs=[pl.BlockSpec(memory_space=pltpu.VMEM)] * 2,
        out_shape=(
            jax.ShapeDtypeStruct((tokens, groups * GSIZE), BF),
            jax.ShapeDtypeStruct((tokens, groups), F32),
        ),
        compiler_params=pltpu.CompilerParams(vmem_limit_bytes=32 << 20),
    )(back)


def finish_kernel(s_ref, q_ref, x_ref, o_ref):
    o_ref[0] = q_ref[0]
    grad = x_ref[0].astype(F32)
    o_ref[1] = (grad * s_ref[2].astype(F32)).astype(BF)
    o_ref[2] = (grad * s_ref[1].astype(F32)).astype(BF)


def finish(saved, d_query, grad_x):
    _, rows, width = saved.shape
    parts, _, own = grad_x.shape
    wide = pl.BlockSpec((3, rows, own), lambda t: (0, 0, t))
    one = pl.BlockSpec((1, rows, own), lambda t: (t, 0, 0))
    return pl.pallas_call(
        finish_kernel,
        grid=(parts,),
        in_specs=[wide, one, one],
        out_specs=wide,
        out_shape=jax.ShapeDtypeStruct(saved.shape, BF),
    )(saved, d_query, grad_x)


def swap(x, axis):
    return lax.all_to_all(x, axis, split_axis=0, concat_axis=0, tiled=True)


def per_device(saved_rows, grad_out, conv_out, filters):
    saved = saved_rows.transpose(1, 0, 2)
    _, rows, width = saved.shape
    tokens, own = grad_out.shape
    parts = width // own
    arrived = swap(pack_rows(saved, parts), "tp")
    spread, d_query = pack_groups(arrived, grad_out, conv_out, filters)
    signals, d_query = lax.optimization_barrier((swap(spread, "ctx"), d_query))
    groups = own // GSIZE
    home_q = swap(d_query.reshape(parts, rows, own), "tp")
    answer = correlate(signals.reshape(groups // 2, 2, OUT_ROWS, tokens))
    back = swap(answer.reshape(groups, BACK_ROWS, tokens), "ctx")
    grad_x, d_filters = unpack_groups(back)
    home_x = swap(grad_x.reshape(parts, rows, own), "tp")
    d_saved = finish(saved, home_q, home_x)
    return (d_saved.transpose(1, 0, 2), d_filters)


def solution(mesh):
    placed = (P(("ctx", "tp"), None, None), P("ctx", "tp"), P("ctx", "tp"), P("ctx", "tp"))
    return jax.shard_map(
        per_device,
        mesh=mesh,
        in_specs=placed,
        out_specs=(P(("ctx", "tp"), None, None), P("ctx", "tp")),
        check_vma=False,
    )
```

time: 228 us -> 185 us (0.81)
  blocking collectives: 0 us -> 141 us
  waiting for transfers between devices: 106 us -> 13.1 us
  starting transfers between devices: 59.1 us -> 3.47 us
  Pallas kernels: 45 us -> 26 us
  local copies, waits for them, and re-layouts: 12.2 us -> 0.01 us
  other arithmetic: 4.3 us -> 0 us
    all_to_all x0 -> x4, blocking collectives: none -> 141 us  [swap(): return lax.all_to_all(x, axis, split_axis=0, concat_axis=0, tiled=True)]
    all_to_all x6 -> x1, waiting for transfers between devices: 106 us -> 13.1 us  [swap(): return lax.all_to_all(x, axis, split_axis=0, concat_axis=0, tiled=True)]
    all_to_all x6 -> x1, starting transfers between devices: 59.1 us -> 3.47 us  [swap(): return lax.all_to_all(x, axis, split_axis=0, concat_axis=0, tiled=True)]
    pallas_call x2 -> x5, Pallas kernels: 45 us -> 26 us  [the longest x1 16.7 us: correlate(): pl.pallas_call(correlate_kernel, in_specs=[pl.BlockSpec(memory_space=pltp...]
    another operation x5 -> x0, local copies, waits for them, and re-layouts: 4.5 us -> none  [the longest x1 1.55 us: per_device(): jnp.stack([x.reshape(rows, parts, own).transpose(1, 0, 2) for x in (saved...]
    convert_element_type x3 -> x0, local copies, waits for them, and re-layouts: 4.09 us -> none  [the longest x2 3.71 us: per_device(): grad_rows = grad_rows.astype(F32)]
  transfers between devices with their start and end apart: 6 -> 1, of which waited for: 5 -> 1; matrix products, arithmetic and copies ran while one was open for 2% -> 0% of each run, Pallas kernels for 11% -> 1%
where the time goes in v1:
time: 185 us; the launch traced here: 184 us
  blocking collectives  141 us (76%)
  Pallas kernels  26 us (14%)
  waiting for transfers between devices  13.1 us (7%)
  starting transfers between devices  3.47 us (2%)
    all_to_all x4, blocking collectives, swap(): return lax.all_to_all(x, axis, split_axis=0, concat_axis=0, tiled=True)  141 us
    pallas_call x1, Pallas kernels, correlate(): pl.pallas_call(correlate_kernel, in_specs=[pl.BlockSpec(memory_space=pltp...  16.7 us
    all_to_all x1, waiting for transfers between devices, swap(): return lax.all_to_all(x, axis, split_axis=0, concat_axis=0, tiled=True)  13.1 us
    pallas_call x1, Pallas kernels, finish(): pl.pallas_call(finish_kernel, grid=(parts,), in_specs=[wide, one, one], o...  3.83 us
  transfers between devices with their start and end apart: 1, of which 1 were waited for; matrix products, arithmetic and copies ran while one was open for 0% of the time, Pallas kernels for 1%

profile of v1, /device:TPU:1, one launch (start us, length us, event | category | flops | bytes accessed | tf_op | source)
XLA Modules:
  0.0 184.0 jit_solution(13897361009912067684)
XLA Ops:
  0.6 3.5 %shard_map.59 = bf16[4,2,32,2048]{3,2,1,0:T(8,128)(2,1)} custom-call(bf16[3,32,8192]{2,1,0:T(8,128)(2,1)} %bitcast.9), custom_call_target="tpu_custom_call" | custom-call | tf_op jit(solution)/shard_map/pallas_call | solution.py:24
  4.1 0.0 copy-start
  4.1 0.0 copy-start.1
  4.1 0.0 copy-start.2
  4.1 32.5 %all_to_all.25.a_ref = bf16[4,2,32,2048]{3,2,1,0:T(8,128)(2,1)S(1)} all-to-all(bf16[4,2,32,2048]{3,2,1,0:T(8,128)(2,1)} %shard_map.59), channel_id=1, replica_groups=mesh['ctx'=128,'tp'=4] {'tp'}, dimensions={0} | all-to-all | bytes 2097152 | tf_op jit(solution)/shard_map/all_to_all | solution.py:217
  36.7 0.0 copy-done
  36.7 0.0 copy-done.1
  36.7 0.0 copy-done.2
  36.7 1.1 shard_map.60
  37.8 56.0 %all_to_all.26 = bf16[128,40,128]{2,1,0:T(8,128)(2,1)S(1)} all-to-all(bf16[128,40,128]{2,1,0:T(8,128)(2,1)S(1)} %get-tuple-element.8), channel_id=1, replica_groups=mesh['ctx'=128,'tp'=4] {'ctx'}, dimensions={0} | all-to-all | bytes 2621440 | tf_op jit(solution)/shard_map/all_to_all | solution.py:217
  93.7 16.7 %shard_map.61 = bf16[64,2,24,128]{3,2,1,0:T(8,128)(2,1)S(1)} custom-call(bf16[64,2,40,128]{3,2,1,0:T(8,128)(2,1)S(1)} %bitcast.6), custom_call_target="tpu_custom_call" | custom-call | flops 21474836480 | bytes 67108864 | tf_op jit(solution)/shard_map/pallas_call | solution.py:150
  110.4 35.6 %all_to_all.27.b_ref = bf16[128,24,128]{2,1,0:T(8,128)(2,1)S(1)} all-to-all(bf16[128,24,128]{2,1,0:T(8,128)(2,1)S(1)} %bitcast.7), channel_id=1, replica_groups=mesh['ctx'=128,'tp'=4] {'ctx'}, dimensions={0} | all-to-all | bytes 1572864 | tf_op jit(solution)/shard_map/all_to_all | solution.py:217
  146.0 3.5 %all-to-all-start.2 = ((bf16[4,32,2048]{2,1,0:T(8,128)(2,1)}), bf16[4,32,2048]{2,1,0:T(8,128)(2,1)S(1)}, u32[]{:S(2)}, u32[]{:S(2)}) async-start(bf16[4,32,2048]{2,1,0:T(8,128)(2,1)} %bitcast.1), calls=%async_computation.2 | async-start | bytes 1048576 | tf_op jit(solution)/shard_map/all_to_all | solution.py:217
  149.5 0.9 shard_map.62
  150.4 13.1 %all-to-all-done.2.q_ref = bf16[4,32,2048]{2,1,0:T(8,128)(2,1)S(1)} async-done(((bf16[4,32,2048]{2,1,0:T(8,128)(2,1)}), bf16[4,32,2048]{2,1,0:T(8,128)(2,1)S(1)}, u32[]{:S(2)}, u32[]{:S(2)}) %all-to-all-start.2) | async-done | bytes 524320 | tf_op jit(solution)/shard_map/all_to_all | solution.py:217
  163.5 0.0 copy-start.3
  163.5 16.6 %all_to_all.28.x_ref = bf16[4,32,2048]{2,1,0:T(8,128)(2,1)} all-to-all(bf16[4,32,2048]{2,1,0:T(8,128)(2,1)S(1)} %bitcast.8), channel_id=1, replica_groups=mesh['ctx'=128,'tp'=4] {'tp'}, dimensions={0} | all-to-all | bytes 1048576 | tf_op jit(solution)/shard_map/all_to_all | solution.py:217
  180.1 0.0 copy-done.3
  180.1 3.8 %shard_map.63 = bf16[3,32,8192]{2,1,0:T(8,128)(2,1)} custom-call(bf16[3,32,8192]{2,1,0:T(8,128)(2,1)} %bitcast.10, bf16[4,32,2048]{2,1,0:T(8,128)(2,1)} %copy-done.3, bf16[4,32,2048]{2,1,0:T(8,128)(2,1)} %all_to_all.28.x_ref), custom_call_target="tpu_custom_call" | custom-call | tf_op jit(solution)/shard_map/pallas_call | solution.py:207
Async XLA Ops:
  4.1 32.5 %copy-start = (bf16[128,2048]{1,0:T(8,128)(2,1)S(1)}, bf16[128,2048]{1,0:T(8,128)(2,1)}, u32[]{:S(2)}) copy-start(bf16[128,2048]{1,0:T(8,128)(2,1)} %g_ref.1) | copy-start | bytes 1572868
  4.1 32.5 %copy-start.1 = (bf16[128,2048]{1,0:T(8,128)(2,1)S(1)}, bf16[128,2048]{1,0:T(8,128)(2,1)}, u32[]{:S(2)}) copy-start(bf16[128,2048]{1,0:T(8,128)(2,1)} %c_ref.1) | copy-start | bytes 1572868
  4.1 32.5 %copy-start.2 = (f32[128,128]{1,0:T(8,128)S(1)}, f32[128,128]{1,0:T(8,128)}, u32[]{:S(2)}) copy-start(f32[128,128]{1,0:T(8,128)} %h_ref.1) | copy-start | bytes 196612
  146.0 17.5 %all-to-all-start.2 = ((bf16[4,32,2048]{2,1,0:T(8,128)(2,1)}), bf16[4,32,2048]{2,1,0:T(8,128)(2,1)S(1)}, u32[]{:S(2)}, u32[]{:S(2)}) async-start(bf16[4,32,2048]{2,1,0:T(8,128)(2,1)} %bitcast.1), calls=%async_computation.2 | async-start | bytes 1048576 | tf_op jit(solution)/shard_map/all_to_all | solution.py:217
  163.5 16.6 %copy-start.3 = (bf16[4,32,2048]{2,1,0:T(8,128)(2,1)}, bf16[4,32,2048]{2,1,0:T(8,128)(2,1)S(1)}, u32[]{:S(2)}) copy-start(bf16[4,32,2048]{2,1,0:T(8,128)(2,1)S(1)} %all-to-all-done.2.q_ref) | copy-start | bytes 1572868

commit v2 on v1

--- a/solution.py
+++ b/solution.py
@@ -13,53 +13,65 @@
 BF = jnp.bfloat16
 
 
-def pack_rows_kernel(s_ref, o_ref):
-    o_ref[0, 0] = s_ref[0]
-    o_ref[0, 1] = (s_ref[1].astype(F32) * s_ref[2].astype(F32)).astype(BF)
-
-
-def pack_rows(saved, parts):
+def pack_rows_kernel(me_ref, s_ref, *o_refs):
+    parts = len(o_refs)
+    own = o_refs[0].shape[2]
+    for k, o_ref in enumerate(o_refs):
+        lanes = pl.ds(pl.multiple_of((me_ref[0] + k) % parts * own, own), own)
+        o_ref[0] = s_ref[0, :, lanes]
+        o_ref[1] = (s_ref[1, :, lanes].astype(F32) * s_ref[2, :, lanes].astype(F32)).astype(BF)
+
+
+def pack_rows(me, saved, parts):
     _, rows, width = saved.shape
-    own = width // parts
+    shape = jax.ShapeDtypeStruct((2, rows, width // parts), BF)
     return pl.pallas_call(
         pack_rows_kernel,
-        grid=(parts,),
-        in_specs=[pl.BlockSpec((3, rows, own), lambda t: (0, 0, t))],
-        out_specs=pl.BlockSpec((1, 2, rows, own), lambda t: (t, 0, 0, 0)),
-        out_shape=jax.ShapeDtypeStruct((parts, 2, rows, own), BF),
-    )(saved)
-
-
-def pack_groups_kernel(a_ref, g_ref, c_ref, h_ref, o_ref, q_ref):
+        in_specs=[
+            pl.BlockSpec(memory_space=pltpu.SMEM),
+            pl.BlockSpec(memory_space=pltpu.VMEM),
+        ],
+        out_specs=[pl.BlockSpec(memory_space=pltpu.VMEM)] * parts,
+        out_shape=[shape] * parts,
+        compiler_params=pltpu.CompilerParams(vmem_limit_bytes=32 << 20),
+    )(me, saved)
+
+
+def pack_groups_kernel(me_ref, g_ref, c_ref, h_ref, *refs):
+    *a_refs, o_ref, q_ref, s_ref = refs
+    parts = len(a_refs)
     tokens, span = g_ref.shape
+    rows = tokens // parts
     count = span // GSIZE
     grad = g_ref[...].astype(F32)
     q_ref[...] = (grad * c_ref[...].astype(F32)).astype(BF)
-    query = a_ref[:, 0].reshape(tokens, span).astype(F32)
-    delta = (query * grad).astype(BF)
+    for k, a_ref in enumerate(a_refs):
+        at = pl.multiple_of((me_ref[0] + parts - k) % parts * rows, rows)
+        s_ref[0, pl.ds(at, rows), :] = a_ref[0]
+        s_ref[1, pl.ds(at, rows), :] = a_ref[1]
+    delta = (s_ref[0].astype(F32) * grad).astype(BF)
     o_ref[:, pl.ds(0, GSIZE), :] = delta.T.reshape(count, GSIZE, tokens)
-    mixed = a_ref[:, 1].reshape(tokens, span)
-    o_ref[:, pl.ds(GSIZE, GSIZE), :] = mixed.T.reshape(count, GSIZE, tokens)
+    o_ref[:, pl.ds(GSIZE, GSIZE), :] = s_ref[1].T.reshape(count, GSIZE, tokens)
     taps = h_ref[...].T
     o_ref[:, pl.ds(2 * GSIZE, 8), :] = jnp.broadcast_to(
         taps[:, None, :], (count, 8, tokens)
     ).astype(BF)
 
 
-def pack_groups(arrived, grad_out, conv_out, filters):
-    parts, _, rows, own = arrived.shape
-    tokens = parts * rows
-    groups = own // GSIZE
+def pack_groups(me, arrived, grad_out, conv_out, filters):
+    tokens, own = grad_out.shape
+    vmem = pl.BlockSpec(memory_space=pltpu.VMEM)
     return pl.pallas_call(
         pack_groups_kernel,
-        in_specs=[pl.BlockSpec(memory_space=pltpu.VMEM)] * 4,
-        out_specs=[pl.BlockSpec(memory_space=pltpu.VMEM)] * 2,
+        in_specs=[pl.BlockSpec(memory_space=pltpu.SMEM)] + [vmem] * (3 + len(arrived)),
+        out_specs=[vmem] * 2,
         out_shape=(
-            jax.ShapeDtypeStruct((groups, OUT_ROWS, tokens), BF),
+            jax.ShapeDtypeStruct((own // GSIZE, OUT_ROWS, tokens), BF),
             jax.ShapeDtypeStruct((tokens, own), BF),
         ),
+        scratch_shapes=[pltpu.VMEM((2, tokens, own), BF)],
         compiler_params=pltpu.CompilerParams(vmem_limit_bytes=32 << 20),
-    )(arrived, grad_out, conv_out, filters)
+    )(me, grad_out, conv_out, filters, *arrived)
 
 
 def correlate_kernel(x_ref, o_ref, d_ref, m_ref, t_ref, f_ref, w_ref, qa_ref, qb_ref, l_ref):
@@ -169,52 +181,80 @@
     )(signals)
 
 
-def unpack_groups_kernel(b_ref, x_ref, h_ref):
+def unpack_groups_kernel(me_ref, b_ref, *refs):
+    *x_refs, h_ref, s_ref = refs
+    parts = len(x_refs)
     groups = b_ref.shape[0]
     tokens = b_ref.shape[2]
-    x_ref[...] = b_ref[:, :GSIZE].reshape(groups * GSIZE, tokens).T
+    rows = tokens // parts
+    s_ref[...] = b_ref[:, :GSIZE].reshape(groups * GSIZE, tokens).T
+    for k, x_ref in enumerate(x_refs):
+        at = pl.multiple_of((me_ref[0] + k) % parts * rows, rows)
+        x_ref[...] = s_ref[pl.ds(at, rows), :]
     tail = b_ref[:, GSIZE:].astype(F32)
     row = lax.broadcasted_iota(jnp.int32, tail.shape, 1)
     h_ref[...] = jnp.sum(jnp.where(row < 2, tail, 0.0), axis=1).T
 
 
-def unpack_groups(back):
+def unpack_groups(me, back, parts):
     groups, _, tokens = back.shape
+    vmem = pl.BlockSpec(memory_space=pltpu.VMEM)
+    chunk = jax.ShapeDtypeStruct((tokens // parts, groups * GSIZE), BF)
     return pl.pallas_call(
         unpack_groups_kernel,
-        in_specs=[pl.BlockSpec(memory_space=pltpu.VMEM)],
-        out_specs=[pl.BlockSpec(memory_space=pltpu.VMEM)] * 2,
-        out_shape=(
-            jax.ShapeDtypeStruct((tokens, groups * GSIZE), BF),
-            jax.ShapeDtypeStruct((tokens, groups), F32),
+        in_specs=[pl.BlockSpec(memory_space=pltpu.SMEM), vmem],
+        out_specs=[vmem] * (parts + 1),
+        out_shape=[chunk] * parts + [jax.ShapeDtypeStruct((tokens, groups), F32)],
+        scratch_shapes=[pltpu.VMEM((tokens, groups * GSIZE), BF)],
+        compiler_params=pltpu.CompilerParams(vmem_limit_bytes=32 << 20),
+    )(me, back)
+
+
+def finish_kernel(me_ref, s_ref, q_ref, *refs):
+    *x_refs, o_ref = refs
+    o_ref[0] = q_ref[0]
+    for k, x_ref in enumerate(x_refs):
+
+        @pl.when(pl.program_id(0) == k)
+        def _():
+            grad = x_ref[...].astype(F32)
+            o_ref[1] = (grad * s_ref[2].astype(F32)).astype(BF)
+            o_ref[2] = (grad * s_ref[1].astype(F32)).astype(BF)
+
+
+def finish(me, saved, d_query, grad_x):
+    _, rows, width = saved.shape
+    parts = len(grad_x)
+    own = width // parts
+
+    def source(k, me_ref):
+        return (me_ref[0] + parts - k) % parts
+
+    wide = pl.BlockSpec((3, rows, own), lambda k, m: (0, 0, source(k, m)))
+    one = pl.BlockSpec((1, rows, own), lambda k, m: (source(k, m), 0, 0))
+    whole = pl.BlockSpec((rows, own), lambda k, m: (0, 0))
+    return pl.pallas_call(
+        finish_kernel,
+        grid_spec=pltpu.PrefetchScalarGridSpec(
+            num_scalar_prefetch=1,
+            grid=(parts,),
+            in_specs=[wide, one] + [whole] * parts,
+            out_specs=wide,
         ),
-        compiler_params=pltpu.CompilerParams(vmem_limit_bytes=32 << 20),
-    )(back)
-
-
-def finish_kernel(s_ref, q_ref, x_ref, o_ref):
-    o_ref[0] = q_ref[0]
-    grad = x_ref[0].astype(F32)
-    o_ref[1] = (grad * s_ref[2].astype(F32)).astype(BF)
-    o_ref[2] = (grad * s_ref[1].astype(F32)).astype(BF)
-
-
-def finish(saved, d_query, grad_x):
-    _, rows, width = saved.shape
-    parts, _, own = grad_x.shape
-    wide = pl.BlockSpec((3, rows, own), lambda t: (0, 0, t))
-    one = pl.BlockSpec((1, rows, own), lambda t: (t, 0, 0))
-    return pl.pallas_call(
-        finish_kernel,
-        grid=(parts,),
-        in_specs=[wide, one, one],
-        out_specs=wide,
         out_shape=jax.ShapeDtypeStruct(saved.shape, BF),
-    )(saved, d_query, grad_x)
+    )(me, saved, d_query, *grad_x)
 
 
 def swap(x, axis):
     return lax.all_to_all(x, axis, split_axis=0, concat_axis=0, tiled=True)
+
+
+def shift(chunks, axis):
+    size = len(chunks)
+    return [chunks[0]] + [
+        lax.ppermute(chunks[k], axis, [(i, (i + k) % size) for i in range(size)])
+        for k in range(1, size)
+    ]
 
 
 def per_device(saved_rows, grad_out, conv_out, filters):
@@ -222,16 +262,17 @@
     _, rows, width = saved.shape
     tokens, own = grad_out.shape
     parts = width // own
-    arrived = swap(pack_rows(saved, parts), "tp")
-    spread, d_query = pack_groups(arrived, grad_out, conv_out, filters)
+    groups = own // GSIZE
+    me = lax.axis_index("tp").reshape(1)
+    arrived = shift(pack_rows(me, saved, parts), "tp")
+    spread, d_query = pack_groups(me, arrived, grad_out, conv_out, filters)
     signals, d_query = lax.optimization_barrier((swap(spread, "ctx"), d_query))
-    groups = own // GSIZE
     home_q = swap(d_query.reshape(parts, rows, own), "tp")
     answer = correlate(signals.reshape(groups // 2, 2, OUT_ROWS, tokens))
+    answer, home_q = lax.optimization_barrier((answer, home_q))
     back = swap(answer.reshape(groups, BACK_ROWS, tokens), "ctx")
-    grad_x, d_filters = unpack_groups(back)
-    home_x = swap(grad_x.reshape(parts, rows, own), "tp")
-    d_saved = finish(saved, home_q, home_x)
+    *grad_x, d_filters = unpack_groups(me, back, parts)
+    d_saved = finish(me, saved, home_q, shift(grad_x, "tp"))
     return (d_saved.transpose(1, 0, 2), d_filters)
 
 

time: 185 us -> 168 us (0.908)
  blocking collectives: 141 us -> 90.1 us
  starting transfers between devices: 3.47 us -> 31.3 us
  waiting for transfers between devices: 13.1 us -> 20.3 us
  Pallas kernels: 26 us -> 22.8 us
  local copies, waits for them, and re-layouts: 0.01 us -> 2.69 us
    all_to_all x4 -> x2, blocking collectives: 141 us -> 90.1 us  [swap(): return lax.all_to_all(x, axis, split_axis=0, concat_axis=0, tiled=True)]
    ppermute x0 -> x6, starting transfers between devices: none -> 23.7 us  [shift(): lax.ppermute(chunks[k], axis, [(i, (i + k) % size) for i in range(size)])]
    ppermute x0 -> x6, waiting for transfers between devices: none -> 20.3 us  [shift(): lax.ppermute(chunks[k], axis, [(i, (i + k) % size) for i in range(size)])]
    all_to_all x1, waiting for transfers between devices: 13.1 us -> 0.01 us  [swap(): return lax.all_to_all(x, axis, split_axis=0, concat_axis=0, tiled=True)]
    all_to_all x1, starting transfers between devices: 3.47 us -> 7.66 us  [swap(): return lax.all_to_all(x, axis, split_axis=0, concat_axis=0, tiled=True)]
    pallas_call x2, Pallas kernels: 7.35 us -> 4.06 us  [the longest x1 3.93 us: finish(): pl.pallas_call(finish_kernel, grid_spec=pltpu.PrefetchScalarGridSpec(num_...]
    unnamed x8 -> x18, local copies, waits for them, and re-layouts: 0.01 us -> 2.69 us
  transfers between devices with their start and end apart: 1 -> 7, of which waited for: 1 -> 4; matrix products, arithmetic and copies ran while one was open for 0% -> 0% of each run, Pallas kernels for 1% -> 10%
where the time goes in v2:
time: 168 us
  blocking collectives  90.1 us (54%)
  starting transfers between devices  31.3 us (19%)
  Pallas kernels  22.8 us (14%)
  waiting for transfers between devices  20.3 us (12%)
  local copies, waits for them, and re-layouts  2.69 us (2%)
    all_to_all x2, blocking collectives, swap(): return lax.all_to_all(x, axis, split_axis=0, concat_axis=0, tiled=True)  90.1 us
    ppermute x6, starting transfers between devices, shift(): lax.ppermute(chunks[k], axis, [(i, (i + k) % size) for i in range(size)])  23.7 us
    ppermute x6, waiting for transfers between devices, shift(): lax.ppermute(chunks[k], axis, [(i, (i + k) % size) for i in range(size)])  20.3 us
    pallas_call x1, Pallas kernels, correlate(): pl.pallas_call(correlate_kernel, in_specs=[pl.BlockSpec(memory_space=pltp...  16.7 us
    all_to_all x1, starting transfers between devices, swap(): return lax.all_to_all(x, axis, split_axis=0, concat_axis=0, tiled=True)  7.66 us
    pallas_call x1, Pallas kernels, finish(): pl.pallas_call(finish_kernel, grid_spec=pltpu.PrefetchScalarGridSpec(num_...  3.93 us
  transfers between devices with their start and end apart: 7, of which 4 were waited for; matrix products, arithmetic and copies ran while one was open for 0% of the time, Pallas kernels for 10%

profile of v2, /device:TPU:1, one launch (start us, length us, event | category | flops | bytes accessed | tf_op | source)
XLA Modules:
  0.0 167.9 jit_solution(7235223672176561141)
XLA Ops:
  0.6 0.0 copy-start
  0.6 1.4 copy-done
  2.1 0.1 shard_map.59
  2.2 5.0 %collective-permute-start = (bf16[2,32,2048]{2,1,0:T(8,128)(2,1)S(1)}, bf16[2,32,2048]{2,1,0:T(8,128)(2,1)S(1)}, u32[]{:S(2)}, u32[]{:S(2)}) collective-permute-start(bf16[2,32,2048]{2,1,0:T(8,128)(2,1)S(1)} %get-tuple-element.18), channel_id=1, source_target_pairs={{0,1},{1,2},{2,3},{3,0},{4,5},{5,6},{6,7},{7,4},{8,9},{9,10},{10,1... | collective-permute-start | bytes 786440 | tf_op jit(solution)/shard_map/ppermute | solution.py:255
  7.2 5.8 %collective-permute-start.1 = (bf16[2,32,2048]{2,1,0:T(8,128)(2,1)S(1)}, bf16[2,32,2048]{2,1,0:T(8,128)(2,1)S(1)}, u32[]{:S(2)}, u32[]{:S(2)}) collective-permute-start(bf16[2,32,2048]{2,1,0:T(8,128)(2,1)S(1)} %get-tuple-element.19), channel_id=1, source_target_pairs={{0,2},{1,3},{2,0},{3,1},{4,6},{5,7},{6,4},{7,5},{8,10},{9,11},{10,... | collective-permute-start | bytes 786440 | tf_op jit(solution)/shard_map/ppermute | solution.py:255
  13.0 2.2 %collective-permute-start.2 = (bf16[2,32,2048]{2,1,0:T(8,128)(2,1)S(1)}, bf16[2,32,2048]{2,1,0:T(8,128)(2,1)S(1)}, u32[]{:S(2)}, u32[]{:S(2)}) collective-permute-start(bf16[2,32,2048]{2,1,0:T(8,128)(2,1)S(1)} %get-tuple-element.20), channel_id=1, source_target_pairs={{0,3},{1,0},{2,1},{3,2},{4,7},{5,4},{6,5},{7,6},{8,11},{9,8},{10,9... | collective-permute-start | bytes 786440 | tf_op jit(solution)/shard_map/ppermute | solution.py:255
  15.2 0.0 collective-permute-done.refs_1_
  15.2 13.7 %collective-permute-done.1.refs_2_ = bf16[2,32,2048]{2,1,0:T(8,128)(2,1)S(1)} collective-permute-done((bf16[2,32,2048]{2,1,0:T(8,128)(2,1)S(1)}, bf16[2,32,2048]{2,1,0:T(8,128)(2,1)S(1)}, u32[]{:S(2)}, u32[]{:S(2)}) %collective-permute-start.1) | collective-permute-done | bytes 262176 | tf_op jit(solution)/shard_map/ppermute | solution.py:255
  28.8 1.0 collective-permute-done.2.refs_3_
  29.8 1.1 shard_map.60
  31.0 54.0 %all_to_all.15 = bf16[128,40,128]{2,1,0:T(8,128)(2,1)S(1)} all-to-all(bf16[128,40,128]{2,1,0:T(8,128)(2,1)S(1)} %get-tuple-element.21), channel_id=1, replica_groups=mesh['ctx'=128,'tp'=4] {'ctx'}, dimensions={0} | all-to-all | bytes 2621440 | tf_op jit(solution)/shard_map/all_to_all | solution.py:249
  85.0 7.7 %all-to-all-start.1 = ((bf16[4,32,2048]{2,1,0:T(8,128)(2,1)}), bf16[4,32,2048]{2,1,0:T(8,128)(2,1)S(1)}, u32[]{:S(2)}, u32[]{:S(2)}) async-start(bf16[4,32,2048]{2,1,0:T(8,128)(2,1)} %bitcast.3), calls=%async_computation.1 | async-start | bytes 1048576 | tf_op jit(solution)/shard_map/all_to_all | solution.py:249
  92.6 16.7 %shard_map.61 = bf16[64,2,24,128]{3,2,1,0:T(8,128)(2,1)S(1)} custom-call(bf16[64,2,40,128]{3,2,1,0:T(8,128)(2,1)S(1)} %bitcast.8), custom_call_target="tpu_custom_call" | custom-call | flops 21474836480 | bytes 67108864 | tf_op jit(solution)/shard_map/pallas_call | solution.py:162
  109.3 0.0 all-to-all-done.1.q_ref
  109.3 36.0 %all_to_all.16.b_ref = bf16[128,24,128]{2,1,0:T(8,128)(2,1)S(1)} all-to-all(bf16[128,24,128]{2,1,0:T(8,128)(2,1)S(1)} %bitcast.9), channel_id=1, replica_groups=mesh['ctx'=128,'tp'=4] {'ctx'}, dimensions={0} | all-to-all | bytes 1572864 | tf_op jit(solution)/shard_map/all_to_all | solution.py:249
  145.4 0.9 shard_map.62
  146.3 0.6 copy-done.3
  146.9 3.6 %collective-permute-start.3 = (bf16[32,2048]{1,0:T(8,128)(2,1)S(1)}, bf16[32,2048]{1,0:T(8,128)(2,1)S(1)}, u32[]{:S(2)}, u32[]{:S(2)}) collective-permute-start(bf16[32,2048]{1,0:T(8,128)(2,1)S(1)} %get-tuple-element.28), channel_id=1, source_target_pairs={{0,1},{1,2},{2,3},{3,0},{4,5},{5,6},{6,7},{7,4},{8,9},{9,10},{10,1... | collective-permute-start | bytes 393224 | tf_op jit(solution)/shard_map/ppermute | solution.py:255
  150.6 4.0 %collective-permute-start.4 = (bf16[32,2048]{1,0:T(8,128)(2,1)S(1)}, bf16[32,2048]{1,0:T(8,128)(2,1)S(1)}, u32[]{:S(2)}, u32[]{:S(2)}) collective-permute-start(bf16[32,2048]{1,0:T(8,128)(2,1)S(1)} %get-tuple-element.29), channel_id=1, source_target_pairs={{0,2},{1,3},{2,0},{3,1},{4,6},{5,7},{6,4},{7,5},{8,10},{9,11},{10,... | collective-permute-start | bytes 393224 | tf_op jit(solution)/shard_map/ppermute | solution.py:255
  154.6 3.1 %collective-permute-start.5 = (bf16[32,2048]{1,0:T(8,128)(2,1)S(1)}, bf16[32,2048]{1,0:T(8,128)(2,1)S(1)}, u32[]{:S(2)}, u32[]{:S(2)}) collective-permute-start(bf16[32,2048]{1,0:T(8,128)(2,1)S(1)} %get-tuple-element.30), channel_id=1, source_target_pairs={{0,3},{1,0},{2,1},{3,2},{4,7},{5,4},{6,5},{7,6},{8,11},{9,8},{10,9... | collective-permute-start | bytes 393224 | tf_op jit(solution)/shard_map/ppermute | solution.py:255
  157.7 3.6 %collective-permute-done.4.refs_2_ = bf16[32,2048]{1,0:T(8,128)(2,1)S(1)} collective-permute-done((bf16[32,2048]{1,0:T(8,128)(2,1)S(1)}, bf16[32,2048]{1,0:T(8,128)(2,1)S(1)}, u32[]{:S(2)}, u32[]{:S(2)}) %collective-permute-start.4) | collective-permute-done | bytes 131104 | tf_op jit(solution)/shard_map/ppermute | solution.py:255
  161.3 2.0 %collective-permute-done.5.refs_3_ = bf16[32,2048]{1,0:T(8,128)(2,1)S(1)} collective-permute-done((bf16[32,2048]{1,0:T(8,128)(2,1)S(1)}, bf16[32,2048]{1,0:T(8,128)(2,1)S(1)}, u32[]{:S(2)}, u32[]{:S(2)}) %collective-permute-start.5) | collective-permute-done | bytes 131104 | tf_op jit(solution)/shard_map/ppermute | solution.py:255
  163.4 0.6 copy-done.8
  164.0 3.9 %shard_map.63 = bf16[3,32,8192]{2,1,0:T(8,128)(2,1)} custom-call(s32[1]{0:T(128)} %bitcast.me_ref, bf16[3,32,8192]{2,1,0:T(8,128)(2,1)} %bitcast.6, bf16[4,32,2048]{2,1,0:T(8,128)(2,1)} %copy-done.5, bf16[32,2048]{1,0:T(8,128)(2,1)} %copy-done.3, bf16[32,2048]{1,0:T(8,128)(2,1)} %copy-done.6, bf16[32,2048]{1,0:T(8,128)(2,1)} %copy-done.7, ...), custom_call_target="tpu_custom_call" | custom-call | tf_op jit(solution)/shard_map/pallas_call | solution.py:236
  (15 shorter events, 0.0 us)
Async XLA Ops:
  0.6 1.4 copy-start
  2.0 27.8 %copy-start.1 = (bf16[128,2048]{1,0:T(8,128)(2,1)S(1)}, bf16[128,2048]{1,0:T(8,128)(2,1)}, u32[]{:S(2)}) copy-start(bf16[128,2048]{1,0:T(8,128)(2,1)} %g_ref.1) | copy-start | bytes 1572868
  2.0 27.8 %copy-start.2 = (bf16[128,2048]{1,0:T(8,128)(2,1)S(1)}, bf16[128,2048]{1,0:T(8,128)(2,1)}, u32[]{:S(2)}) copy-start(bf16[128,2048]{1,0:T(8,128)(2,1)} %c_ref.1) | copy-start | bytes 1572868
  2.0 27.8 %copy-start.4 = (f32[128,128]{1,0:T(8,128)S(1)}, f32[128,128]{1,0:T(8,128)}, u32[]{:S(2)}) copy-start(f32[128,128]{1,0:T(8,128)} %h_ref.1) | copy-start | bytes 196612
  2.2 13.0 %collective-permute-start = (bf16[2,32,2048]{2,1,0:T(8,128)(2,1)S(1)}, bf16[2,32,2048]{2,1,0:T(8,128)(2,1)S(1)}, u32[]{:S(2)}, u32[]{:S(2)}) collective-permute-start(bf16[2,32,2048]{2,1,0:T(8,128)(2,1)S(1)} %get-tuple-element.18), channel_id=1, source_target_pairs={{0,1},{1,2},{2,3},{3,0},{4,5},{5,6},{6,7},{7,4},{8,9},{9,10},{10,1... | collective-permute-start | bytes 786440 | tf_op jit(solution)/shard_map/ppermute | solution.py:255
  7.2 21.7 %collective-permute-start.1 = (bf16[2,32,2048]{2,1,0:T(8,128)(2,1)S(1)}, bf16[2,32,2048]{2,1,0:T(8,128)(2,1)S(1)}, u32[]{:S(2)}, u32[]{:S(2)}) collective-permute-start(bf16[2,32,2048]{2,1,0:T(8,128)(2,1)S(1)} %get-tuple-element.19), channel_id=1, source_target_pairs={{0,2},{1,3},{2,0},{3,1},{4,6},{5,7},{6,4},{7,5},{8,10},{9,11},{10,... | collective-permute-start | bytes 786440 | tf_op jit(solution)/shard_map/ppermute | solution.py:255
  13.0 16.8 %collective-permute-start.2 = (bf16[2,32,2048]{2,1,0:T(8,128)(2,1)S(1)}, bf16[2,32,2048]{2,1,0:T(8,128)(2,1)S(1)}, u32[]{:S(2)}, u32[]{:S(2)}) collective-permute-start(bf16[2,32,2048]{2,1,0:T(8,128)(2,1)S(1)} %get-tuple-element.20), channel_id=1, source_target_pairs={{0,3},{1,0},{2,1},{3,2},{4,7},{5,4},{6,5},{7,6},{8,11},{9,8},{10,9... | collective-permute-start | bytes 786440 | tf_op jit(solution)/shard_map/ppermute | solution.py:255
  85.0 24.3 %all-to-all-start.1 = ((bf16[4,32,2048]{2,1,0:T(8,128)(2,1)}), bf16[4,32,2048]{2,1,0:T(8,128)(2,1)S(1)}, u32[]{:S(2)}, u32[]{:S(2)}) async-start(bf16[4,32,2048]{2,1,0:T(8,128)(2,1)} %bitcast.3), calls=%async_computation.1 | async-start | bytes 1048576 | tf_op jit(solution)/shard_map/all_to_all | solution.py:249
  109.3 54.0 %copy-start.5 = (bf16[4,32,2048]{2,1,0:T(8,128)(2,1)}, bf16[4,32,2048]{2,1,0:T(8,128)(2,1)S(1)}, u32[]{:S(2)}) copy-start(bf16[4,32,2048]{2,1,0:T(8,128)(2,1)S(1)} %all-to-all-done.1.q_ref) | copy-start | bytes 1572868
  146.3 0.6 copy-start.3
  146.9 10.7 %collective-permute-start.3 = (bf16[32,2048]{1,0:T(8,128)(2,1)S(1)}, bf16[32,2048]{1,0:T(8,128)(2,1)S(1)}, u32[]{:S(2)}, u32[]{:S(2)}) collective-permute-start(bf16[32,2048]{1,0:T(8,128)(2,1)S(1)} %get-tuple-element.28), channel_id=1, source_target_pairs={{0,1},{1,2},{2,3},{3,0},{4,5},{5,6},{6,7},{7,4},{8,9},{9,10},{10,1... | collective-permute-start | bytes 393224 | tf_op jit(solution)/shard_map/ppermute | solution.py:255
  150.6 10.7 %collective-permute-start.4 = (bf16[32,2048]{1,0:T(8,128)(2,1)S(1)}, bf16[32,2048]{1,0:T(8,128)(2,1)S(1)}, u32[]{:S(2)}, u32[]{:S(2)}) collective-permute-start(bf16[32,2048]{1,0:T(8,128)(2,1)S(1)} %get-tuple-element.29), channel_id=1, source_target_pairs={{0,2},{1,3},{2,0},{3,1},{4,6},{5,7},{6,4},{7,5},{8,10},{9,11},{10,... | collective-permute-start | bytes 393224 | tf_op jit(solution)/shard_map/ppermute | solution.py:255
  154.6 8.8 %collective-permute-start.5 = (bf16[32,2048]{1,0:T(8,128)(2,1)S(1)}, bf16[32,2048]{1,0:T(8,128)(2,1)S(1)}, u32[]{:S(2)}, u32[]{:S(2)}) collective-permute-start(bf16[32,2048]{1,0:T(8,128)(2,1)S(1)} %get-tuple-element.30), channel_id=1, source_target_pairs={{0,3},{1,0},{2,1},{3,2},{4,7},{5,4},{6,5},{7,6},{8,11},{9,8},{10,9... | collective-permute-start | bytes 393224 | tf_op jit(solution)/shard_map/ppermute | solution.py:255
  157.7 5.7 %copy-start.6 = (bf16[32,2048]{1,0:T(8,128)(2,1)}, bf16[32,2048]{1,0:T(8,128)(2,1)S(1)}, u32[]{:S(2)}) copy-start(bf16[32,2048]{1,0:T(8,128)(2,1)S(1)} %collective-permute-done.3.refs_1_) | copy-start | bytes 393220
  161.3 2.0 %copy-start.7 = (bf16[32,2048]{1,0:T(8,128)(2,1)}, bf16[32,2048]{1,0:T(8,128)(2,1)S(1)}, u32[]{:S(2)}) copy-start(bf16[32,2048]{1,0:T(8,128)(2,1)S(1)} %collective-permute-done.4.refs_2_) | copy-start | bytes 393220
  163.3 0.6 copy-start.8

commit v3 on v2

--- a/solution.py
+++ b/solution.py
@@ -8,7 +8,7 @@
 GSIZE = 16
 B = 128
 OUT_ROWS = 40
-BACK_ROWS = 24
+BACK_ROWS = 8
 F32 = jnp.float32
 BF = jnp.bfloat16
 
@@ -74,6 +74,30 @@
     )(me, grad_out, conv_out, filters, *arrived)
 
 
+def regroup(part, sums, o_ref, tile, half):
+    shape = (16, 8, B)
+    row = lax.broadcasted_iota(jnp.int32, shape, 1)
+    lane = lax.broadcasted_iota(jnp.int32, shape, 2) // 32
+    low, high = part[:, :8], part[:, 8:]
+    fours = [low, jnp.roll(low, 4, axis=1), high, jnp.roll(high, 4, axis=1)]
+    turned = []
+    for d in range(4):
+        mix = fours[(3 + d) % 4]
+        for t in range(3):
+            mix = jnp.where(lane == t, fours[(t + d) % 4], mix)
+        turned.append(mix if d == 0 else jnp.roll(mix, 32 * d, axis=2))
+    coarse = sums.astype(BF).astype(F32)
+    fine = sums - coarse
+    coarse = jnp.broadcast_to(coarse[:, None], shape)
+    fine = jnp.broadcast_to(fine[:, None], shape)
+    rest = jnp.where(row == 4, coarse, jnp.where(row == 5, fine, 0.0))
+    for t in range(4):
+        chunk = turned[(3 - t) % 4]
+        for i in range(3):
+            chunk = jnp.where(lane == i, turned[(i - t) % 4], chunk)
+        o_ref[pl.ds(16 * tile, 16), half, t] = jnp.where(row < 4, chunk, rest).astype(BF)
+
+
 def correlate_kernel(x_ref, o_ref, d_ref, m_ref, t_ref, f_ref, w_ref, qa_ref, qb_ref, l_ref):
     for half in range(2):
         lanes = pl.ds(B * half, B)
@@ -82,32 +106,6 @@
     d_ref[pl.ds(1024, 256), :] = jnp.zeros((256, 256), BF)
     row = lax.broadcasted_iota(jnp.int32, (B, B), 0)
     col = lax.broadcasted_iota(jnp.int32, (B, B), 1)
-
-    flip = jnp.where((row + col) % B == 0, 1.0, 0.0).astype(BF)
-    taps = x_ref[:, :, 2 * GSIZE :].astype(F32).reshape(1024, B).astype(BF)
-    f_ref[...] = jnp.dot(taps, flip, preferred_element_type=F32).reshape(B, 8, B)
-    lower = row >= col
-    w_ref[pl.ds(0, B), pl.ds(B, B)] = jnp.zeros((B, B), BF)
-
-    def build(e, before):
-        line = jnp.broadcast_to(f_ref[pl.ds(e, 1)], (16, 8, B)).reshape(B, B)
-        turned = pltpu.roll(line, 0, 1, stride=1, stride_axis=0)
-        block = jnp.where(lower, turned, before).astype(BF)
-        at = pl.multiple_of(e * B, B)
-        w_ref[pl.ds(at, B), pl.ds(0, B)] = block
-        w_ref[pl.ds(at + B, B), pl.ds(B, B)] = block
-        return turned
-
-    lax.fori_loop(0, B, build, jnp.zeros((B, B), F32), unroll=16)
-    for tile in range(4):
-        count = 64 - 16 * tile
-        left = jnp.concatenate(
-            [d_ref[pl.ds(256 * tile + 16 * u, 256), :] for u in range(count)], axis=1
-        )
-        total = jnp.dot(left, w_ref[pl.ds(0, 256 * count), :], preferred_element_type=F32)
-        for half in range(2):
-            part = total[:, B * half : B * half + B].astype(BF)
-            o_ref[pl.ds(16 * tile, 16), half, pl.ds(0, GSIZE)] = part.reshape(16, GSIZE, B)
 
     mirror = jnp.where(row + col == B - 1, 1.0, 0.0).astype(BF)
     for half in range(2):
@@ -147,15 +145,32 @@
         return carry
 
     lax.fori_loop(0, 64, diagonals, 0, unroll=16)
-    sums = l_ref[...]
-    coarse = sums.astype(BF).astype(F32)
-    fine = sums - coarse
-    shape = (B, 8, B)
-    pick = lax.broadcasted_iota(jnp.int32, shape, 1) == 0
-    both = jnp.where(
-        pick, jnp.broadcast_to(coarse[:, None], shape), jnp.broadcast_to(fine[:, None], shape)
-    )
-    o_ref[:, :, pl.ds(GSIZE, 8)] = both.astype(BF).reshape(64, 2, 8, B)
+    flip = jnp.where((row + col) % B == 0, 1.0, 0.0).astype(BF)
+    taps = x_ref[:, :, 2 * GSIZE :].astype(F32).reshape(1024, B).astype(BF)
+    f_ref[...] = jnp.dot(taps, flip, preferred_element_type=F32).reshape(B, 8, B)
+    lower = row >= col
+    w_ref[pl.ds(0, B), pl.ds(B, B)] = jnp.zeros((B, B), BF)
+
+    def build(e, before):
+        line = jnp.broadcast_to(f_ref[pl.ds(e, 1)], (16, 8, B)).reshape(B, B)
+        turned = pltpu.roll(line, 0, 1, stride=1, stride_axis=0)
+        block = jnp.where(lower, turned, before).astype(BF)
+        at = pl.multiple_of(e * B, B)
+        w_ref[pl.ds(at, B), pl.ds(0, B)] = block
+        w_ref[pl.ds(at + B, B), pl.ds(B, B)] = block
+        return turned
+
+    lax.fori_loop(0, B, build, jnp.zeros((B, B), F32), unroll=16)
+    for tile in range(4):
+        count = 64 - 16 * tile
+        left = jnp.concatenate(
+            [d_ref[pl.ds(256 * tile + 16 * u, 256), :] for u in range(count)], axis=1
+        )
+        total = jnp.dot(left, w_ref[pl.ds(0, 256 * count), :], preferred_element_type=F32)
+        for half in range(2):
+            part = total[:, B * half : B * half + B].reshape(16, GSIZE, B)
+            sums = l_ref[pl.ds(32 * tile + half, 16, stride=2), :]
+            regroup(part, sums, o_ref, tile, half)
 
 
 def correlate(signals):
@@ -163,7 +178,7 @@
         correlate_kernel,
         in_specs=[pl.BlockSpec(memory_space=pltpu.VMEM)],
         out_specs=pl.BlockSpec(memory_space=pltpu.VMEM),
-        out_shape=jax.ShapeDtypeStruct((64, 2, BACK_ROWS, B), BF),
+        out_shape=jax.ShapeDtypeStruct((64, 2, 4, BACK_ROWS, B), BF),
         scratch_shapes=[
             pltpu.VMEM((1280, 256), BF),
             pltpu.VMEM((1024, 256), BF),
@@ -181,68 +196,69 @@
     )(signals)
 
 
-def unpack_groups_kernel(me_ref, b_ref, *refs):
-    *x_refs, h_ref, s_ref = refs
-    parts = len(x_refs)
-    groups = b_ref.shape[0]
-    tokens = b_ref.shape[2]
-    rows = tokens // parts
-    s_ref[...] = b_ref[:, :GSIZE].reshape(groups * GSIZE, tokens).T
-    for k, x_ref in enumerate(x_refs):
-        at = pl.multiple_of((me_ref[0] + k) % parts * rows, rows)
-        x_ref[...] = s_ref[pl.ds(at, rows), :]
-    tail = b_ref[:, GSIZE:].astype(F32)
-    row = lax.broadcasted_iota(jnp.int32, tail.shape, 1)
-    h_ref[...] = jnp.sum(jnp.where(row < 2, tail, 0.0), axis=1).T
-
-
-def unpack_groups(me, back, parts):
-    groups, _, tokens = back.shape
+def finish_kernel(me_ref, s_ref, q_ref, b_ref, o_ref, h_ref, l_ref, d_ref, sem):
+    parts, rows, own = q_ref.shape
+    steps = own // 256
+
+    def send(source, plane, t):
+        lanes = pl.ds(own * t, own)
+        return pltpu.make_async_copy(source, o_ref.at[plane, :, lanes], sem.at[plane, t])
+
+    copies = [send(q_ref.at[t], 0, t) for t in range(parts)]
+    for copy in copies:
+        copy.start()
+    shape = (4 * B, 256)
+    row = lax.broadcasted_iota(jnp.int32, shape, 0)
+    col = lax.broadcasted_iota(jnp.int32, shape, 1)
+    inner = row % B
+    wanted = (inner // 8) * GSIZE + 4 * (row // B) + inner % 8
+    spread = jnp.where((inner % 8 < 4) & (col == wanted), 1.0, 0.0).astype(BF)
+    for t in range(parts):
+        chunk = b_ref[:, t].astype(F32).reshape(B * 8, B).astype(BF).T
+        for i in range(4):
+            for b in range(steps):
+                l_ref[pl.ds((t * steps + b) * rows, rows), pl.ds(B * i, B)] = chunk[
+                    rows * i : rows * i + rows, B * b : B * b + B
+                ]
+        span = steps * rows
+        grad = jnp.dot(
+            l_ref[pl.ds(t * span, span), :], spread, preferred_element_type=F32
+        )
+        for b in range(steps):
+            lanes = pl.ds(own * t + 256 * b, 256)
+            here = grad[b * rows : b * rows + rows]
+            d_ref[0, :, lanes] = (here * s_ref[2, :, lanes].astype(F32)).astype(BF)
+            d_ref[1, :, lanes] = (here * s_ref[1, :, lanes].astype(F32)).astype(BF)
+        for plane in (1, 2):
+            copy = send(d_ref.at[plane - 1, :, pl.ds(own * t, own)], plane, t)
+            copy.start()
+            copies.append(copy)
+    tail = b_ref[:, pl.ds(me_ref[0], 1)].reshape(b_ref.shape[0], 8, B).astype(F32)
+    line = lax.broadcasted_iota(jnp.int32, tail.shape, 1)
+    h_ref[...] = jnp.sum(jnp.where((line == 4) | (line == 5), tail, 0.0), axis=1).T
+    for copy in copies:
+        copy.wait()
+
+
+def finish(me, saved, d_query, back):
+    _, rows, width = saved.shape
+    parts, _, own = d_query.shape
     vmem = pl.BlockSpec(memory_space=pltpu.VMEM)
-    chunk = jax.ShapeDtypeStruct((tokens // parts, groups * GSIZE), BF)
-    return pl.pallas_call(
-        unpack_groups_kernel,
-        in_specs=[pl.BlockSpec(memory_space=pltpu.SMEM), vmem],
-        out_specs=[vmem] * (parts + 1),
-        out_shape=[chunk] * parts + [jax.ShapeDtypeStruct((tokens, groups), F32)],
-        scratch_shapes=[pltpu.VMEM((tokens, groups * GSIZE), BF)],
-        compiler_params=pltpu.CompilerParams(vmem_limit_bytes=32 << 20),
-    )(me, back)
-
-
-def finish_kernel(me_ref, s_ref, q_ref, *refs):
-    *x_refs, o_ref = refs
-    o_ref[0] = q_ref[0]
-    for k, x_ref in enumerate(x_refs):
-
-        @pl.when(pl.program_id(0) == k)
-        def _():
-            grad = x_ref[...].astype(F32)
-            o_ref[1] = (grad * s_ref[2].astype(F32)).astype(BF)
-            o_ref[2] = (grad * s_ref[1].astype(F32)).astype(BF)
-
-
-def finish(me, saved, d_query, grad_x):
-    _, rows, width = saved.shape
-    parts = len(grad_x)
-    own = width // parts
-
-    def source(k, me_ref):
-        return (me_ref[0] + parts - k) % parts
-
-    wide = pl.BlockSpec((3, rows, own), lambda k, m: (0, 0, source(k, m)))
-    one = pl.BlockSpec((1, rows, own), lambda k, m: (source(k, m), 0, 0))
-    whole = pl.BlockSpec((rows, own), lambda k, m: (0, 0))
     return pl.pallas_call(
         finish_kernel,
-        grid_spec=pltpu.PrefetchScalarGridSpec(
-            num_scalar_prefetch=1,
-            grid=(parts,),
-            in_specs=[wide, one] + [whole] * parts,
-            out_specs=wide,
+        in_specs=[pl.BlockSpec(memory_space=pltpu.SMEM), vmem, vmem, vmem],
+        out_specs=[pl.BlockSpec(memory_space=pl.ANY), vmem],
+        out_shape=(
+            jax.ShapeDtypeStruct(saved.shape, BF),
+            jax.ShapeDtypeStruct((B, own // GSIZE), F32),
         ),
-        out_shape=jax.ShapeDtypeStruct(saved.shape, BF),
-    )(me, saved, d_query, *grad_x)
+        scratch_shapes=[
+            pltpu.VMEM((parts * (own // 256) * rows, 4 * B), BF),
+            pltpu.VMEM((2, rows, width), BF),
+            pltpu.SemaphoreType.DMA((3, parts)),
+        ],
+        compiler_params=pltpu.CompilerParams(vmem_limit_bytes=32 << 20),
+    )(me, saved, d_query, back)
 
 
 def swap(x, axis):
@@ -270,9 +286,9 @@
     home_q = swap(d_query.reshape(parts, rows, own), "tp")
     answer = correlate(signals.reshape(groups // 2, 2, OUT_ROWS, tokens))
     answer, home_q = lax.optimization_barrier((answer, home_q))
-    back = swap(answer.reshape(groups, BACK_ROWS, tokens), "ctx")
-    *grad_x, d_filters = unpack_groups(me, back, parts)
-    d_saved = finish(me, saved, home_q, shift(grad_x, "tp"))
+    back = swap(answer.reshape(groups * parts, BACK_ROWS, tokens), ("ctx", "tp"))
+    back = back.reshape(groups, parts, BACK_ROWS, tokens)
+    d_saved, d_filters = finish(me, saved, home_q, back)
     return (d_saved.transpose(1, 0, 2), d_filters)
 
 

time: 168 us -> 158 us (0.940)
  starting transfers between devices: 31.3 us -> 20.6 us
  blocking collectives: 90.1 us -> 100 us
  waiting for transfers between devices: 20.3 us -> 14.6 us
  Pallas kernels: 22.8 us -> 20.3 us
    ppermute x6 -> x3, starting transfers between devices: 23.7 us -> 13 us  [shift(): lax.ppermute(chunks[k], axis, [(i, (i + k) % size) for i in range(size)])]
    all_to_all x2, blocking collectives: 90.1 us -> 100 us  [swap(): return lax.all_to_all(x, axis, split_axis=0, concat_axis=0, tiled=True)]
    ppermute x6 -> x3, waiting for transfers between devices: 20.3 us -> 14.6 us  [shift(): lax.ppermute(chunks[k], axis, [(i, (i + k) % size) for i in range(size)])]
    pallas_call x2 -> x1, Pallas kernels: 4.86 us -> 2.25 us  [finish(): pl.pallas_call(finish_kernel, in_specs=[pl.BlockSpec(memory_space=pltpu.S...]
  transfers between devices with their start and end apart: 7 -> 4, of which waited for: 4 -> 2; matrix products, arithmetic and copies ran while one was open for 0% -> 0% of each run, Pallas kernels for 10% -> 11%
where the time goes in v3:
time: 158 us
  blocking collectives  100 us (63%)
  starting transfers between devices  20.6 us (13%)
  Pallas kernels  20.3 us (13%)
  waiting for transfers between devices  14.6 us (9%)
    all_to_all x2, blocking collectives, swap(): return lax.all_to_all(x, axis, split_axis=0, concat_axis=0, tiled=True)  100 us
    pallas_call x1, Pallas kernels, correlate(): pl.pallas_call(correlate_kernel, in_specs=[pl.BlockSpec(memory_space=pltp...  16.8 us
    ppermute x3, waiting for transfers between devices, shift(): lax.ppermute(chunks[k], axis, [(i, (i + k) % size) for i in range(size)])  14.6 us
    ppermute x3, starting transfers between devices, shift(): lax.ppermute(chunks[k], axis, [(i, (i + k) % size) for i in range(size)])  13 us
    all_to_all x1, starting transfers between devices, swap(): return lax.all_to_all(x, axis, split_axis=0, concat_axis=0, tiled=True)  7.66 us
  transfers between devices with their start and end apart: 4, of which 2 were waited for; matrix products, arithmetic and copies ran while one was open for 0% of the time, Pallas kernels for 11%

profile of v3, /device:TPU:1, one launch (start us, length us, event | category | flops | bytes accessed | tf_op | source)
XLA Modules:
  0.0 157.9 jit_solution(4863047637357664926)
XLA Ops:
  0.6 0.0 copy-start
  0.6 1.4 copy-done
  2.0 0.0 copy-start.2
  2.0 0.0 copy-start.3
  2.0 0.0 copy-start.4
  2.1 0.1 shard_map.59
  2.2 5.0 %collective-permute-start = (bf16[2,32,2048]{2,1,0:T(8,128)(2,1)S(1)}, bf16[2,32,2048]{2,1,0:T(8,128)(2,1)S(1)}, u32[]{:S(2)}, u32[]{:S(2)}) collective-permute-start(bf16[2,32,2048]{2,1,0:T(8,128)(2,1)S(1)} %get-tuple-element.15), channel_id=1, source_target_pairs={{0,1},{1,2},{2,3},{3,0},{4,5},{5,6},{6,7},{7,4},{8,9},{9,10},{10,1... | collective-permute-start | bytes 786440 | tf_op jit(solution)/shard_map/ppermute | solution.py:271
  7.2 5.8 %collective-permute-start.1 = (bf16[2,32,2048]{2,1,0:T(8,128)(2,1)S(1)}, bf16[2,32,2048]{2,1,0:T(8,128)(2,1)S(1)}, u32[]{:S(2)}, u32[]{:S(2)}) collective-permute-start(bf16[2,32,2048]{2,1,0:T(8,128)(2,1)S(1)} %get-tuple-element.16), channel_id=1, source_target_pairs={{0,2},{1,3},{2,0},{3,1},{4,6},{5,7},{6,4},{7,5},{8,10},{9,11},{10,... | collective-permute-start | bytes 786440 | tf_op jit(solution)/shard_map/ppermute | solution.py:271
  13.0 2.2 %collective-permute-start.2 = (bf16[2,32,2048]{2,1,0:T(8,128)(2,1)S(1)}, bf16[2,32,2048]{2,1,0:T(8,128)(2,1)S(1)}, u32[]{:S(2)}, u32[]{:S(2)}) collective-permute-start(bf16[2,32,2048]{2,1,0:T(8,128)(2,1)S(1)} %get-tuple-element.17), channel_id=1, source_target_pairs={{0,3},{1,0},{2,1},{3,2},{4,7},{5,4},{6,5},{7,6},{8,11},{9,8},{10,9... | collective-permute-start | bytes 786440 | tf_op jit(solution)/shard_map/ppermute | solution.py:271
  15.2 0.0 collective-permute-done.refs_1_
  15.2 13.7 %collective-permute-done.1.refs_2_ = bf16[2,32,2048]{2,1,0:T(8,128)(2,1)S(1)} collective-permute-done((bf16[2,32,2048]{2,1,0:T(8,128)(2,1)S(1)}, bf16[2,32,2048]{2,1,0:T(8,128)(2,1)S(1)}, u32[]{:S(2)}, u32[]{:S(2)}) %collective-permute-start.1) | collective-permute-done | bytes 262176 | tf_op jit(solution)/shard_map/ppermute | solution.py:271
  28.8 1.0 collective-permute-done.2.refs_3_
  29.8 0.0 copy-done.2
  29.8 0.0 copy-done.3
  29.8 0.0 copy-done.4
  29.8 1.1 shard_map.60
  31.0 54.0 %all_to_all.15 = bf16[128,40,128]{2,1,0:T(8,128)(2,1)S(1)} all-to-all(bf16[128,40,128]{2,1,0:T(8,128)(2,1)S(1)} %get-tuple-element.18), channel_id=1, replica_groups=mesh['ctx'=128,'tp'=4] {'ctx'}, dimensions={0} | all-to-all | bytes 2621440 | tf_op jit(solution)/shard_map/all_to_all | solution.py:265
  85.0 7.7 %all-to-all-start.1 = ((bf16[4,32,2048]{2,1,0:T(8,128)(2,1)}), bf16[4,32,2048]{2,1,0:T(8,128)(2,1)S(1)}, u32[]{:S(2)}, u32[]{:S(2)}) async-start(bf16[4,32,2048]{2,1,0:T(8,128)(2,1)} %bitcast.3), calls=%async_computation.1 | async-start | bytes 1048576 | tf_op jit(solution)/shard_map/all_to_all | solution.py:265
  92.6 16.8 %shard_map.61 = bf16[64,2,4,8,128]{4,3,2,1,0:T(8,128)(2,1)S(1)} custom-call(bf16[64,2,40,128]{3,2,1,0:T(8,128)(2,1)S(1)} %bitcast.10), custom_call_target="tpu_custom_call" | custom-call | flops 21474836480 | bytes 67108864 | tf_op jit(solution)/shard_map/pallas_call | solution.py:177
  109.4 0.0 copy-start.1
  109.4 0.0 all-to-all-done.1.q_ref
  109.4 46.1 %all_to_all.16 = bf16[512,8,128]{2,1,0:T(8,128)(2,1)S(1)} all-to-all(bf16[512,8,128]{2,1,0:T(8,128)(2,1)S(1)} %bitcast.11), channel_id=1, replica_groups=mesh['ctx'=128,'tp'=4] {'ctx','tp'}, dimensions={0} | all-to-all | bytes 2097152 | tf_op jit(solution)/shard_map/all_to_all | solution.py:265
  155.5 0.0 copy-done.1
  155.5 2.3 %shard_map.62 = (bf16[3,32,8192]{2,1,0:T(8,128)(2,1)}, f32[128,128]{1,0:T(8,128)}) custom-call(s32[1]{0:T(128)} %bitcast.me_ref, bf16[3,32,8192]{2,1,0:T(8,128)(2,1)S(1)} %bitcast.8, bf16[4,32,2048]{2,1,0:T(8,128)(2,1)S(1)} %all-to-all-done.1.q_ref, bf16[128,4,8,128]{3,2,1,0:T(8,128)(2,1)S(1)} %bitcast.9), custom_call_target="tpu_custom_call" | custom-call | tf_op jit(solution)/shard_map/pallas_call | solution.py:247
Async XLA Ops:
  0.6 1.4 copy-start
  2.0 27.8 %copy-start.2 = (bf16[128,2048]{1,0:T(8,128)(2,1)S(1)}, bf16[128,2048]{1,0:T(8,128)(2,1)}, u32[]{:S(2)}) copy-start(bf16[128,2048]{1,0:T(8,128)(2,1)} %g_ref.1) | copy-start | bytes 1572868
  2.0 27.8 %copy-start.3 = (bf16[128,2048]{1,0:T(8,128)(2,1)S(1)}, bf16[128,2048]{1,0:T(8,128)(2,1)}, u32[]{:S(2)}) copy-start(bf16[128,2048]{1,0:T(8,128)(2,1)} %c_ref.1) | copy-start | bytes 1572868
  2.0 27.8 %copy-start.4 = (f32[128,128]{1,0:T(8,128)S(1)}, f32[128,128]{1,0:T(8,128)}, u32[]{:S(2)}) copy-start(f32[128,128]{1,0:T(8,128)} %h_ref.1) | copy-start | bytes 196612
  2.2 13.0 %collective-permute-start = (bf16[2,32,2048]{2,1,0:T(8,128)(2,1)S(1)}, bf16[2,32,2048]{2,1,0:T(8,128)(2,1)S(1)}, u32[]{:S(2)}, u32[]{:S(2)}) collective-permute-start(bf16[2,32,2048]{2,1,0:T(8,128)(2,1)S(1)} %get-tuple-element.15), channel_id=1, source_target_pairs={{0,1},{1,2},{2,3},{3,0},{4,5},{5,6},{6,7},{7,4},{8,9},{9,10},{10,1... | collective-permute-start | bytes 786440 | tf_op jit(solution)/shard_map/ppermute | solution.py:271
  7.2 21.7 %collective-permute-start.1 = (bf16[2,32,2048]{2,1,0:T(8,128)(2,1)S(1)}, bf16[2,32,2048]{2,1,0:T(8,128)(2,1)S(1)}, u32[]{:S(2)}, u32[]{:S(2)}) collective-permute-start(bf16[2,32,2048]{2,1,0:T(8,128)(2,1)S(1)} %get-tuple-element.16), channel_id=1, source_target_pairs={{0,2},{1,3},{2,0},{3,1},{4,6},{5,7},{6,4},{7,5},{8,10},{9,11},{10,... | collective-permute-start | bytes 786440 | tf_op jit(solution)/shard_map/ppermute | solution.py:271
  13.0 16.8 %collective-permute-start.2 = (bf16[2,32,2048]{2,1,0:T(8,128)(2,1)S(1)}, bf16[2,32,2048]{2,1,0:T(8,128)(2,1)S(1)}, u32[]{:S(2)}, u32[]{:S(2)}) collective-permute-start(bf16[2,32,2048]{2,1,0:T(8,128)(2,1)S(1)} %get-tuple-element.17), channel_id=1, source_target_pairs={{0,3},{1,0},{2,1},{3,2},{4,7},{5,4},{6,5},{7,6},{8,11},{9,8},{10,9... | collective-permute-start | bytes 786440 | tf_op jit(solution)/shard_map/ppermute | solution.py:271
  85.0 24.4 %all-to-all-start.1 = ((bf16[4,32,2048]{2,1,0:T(8,128)(2,1)}), bf16[4,32,2048]{2,1,0:T(8,128)(2,1)S(1)}, u32[]{:S(2)}, u32[]{:S(2)}) async-start(bf16[4,32,2048]{2,1,0:T(8,128)(2,1)} %bitcast.3), calls=%async_computation.1 | async-start | bytes 1048576 | tf_op jit(solution)/shard_map/all_to_all | solution.py:265
  109.4 46.1 %copy-start.1 = (bf16[32,3,8192]{2,0,1:T(8,128)(2,1)S(1)}, bf16[32,3,8192]{2,0,1:T(8,128)(2,1)}, u32[]{:S(2)}) copy-start(bf16[32,3,8192]{2,0,1:T(8,128)(2,1)} %param.4) | copy-start | bytes 4718596

commit v4 on v3

--- a/solution.py
+++ b/solution.py
@@ -8,7 +8,7 @@
 GSIZE = 16
 B = 128
 OUT_ROWS = 40
-BACK_ROWS = 8
+BACK_ROWS = 6
 F32 = jnp.float32
 BF = jnp.bfloat16
 
@@ -91,11 +91,16 @@
     coarse = jnp.broadcast_to(coarse[:, None], shape)
     fine = jnp.broadcast_to(fine[:, None], shape)
     rest = jnp.where(row == 4, coarse, jnp.where(row == 5, fine, 0.0))
+    chunks = []
     for t in range(4):
         chunk = turned[(3 - t) % 4]
         for i in range(3):
             chunk = jnp.where(lane == i, turned[(i - t) % 4], chunk)
-        o_ref[pl.ds(16 * tile, 16), half, t] = jnp.where(row < 4, chunk, rest).astype(BF)
+        chunk = jnp.where(row < 4, chunk, rest)
+        chunks.append(chunk if t == 0 else jnp.roll(chunk, 8 - 2 * t, axis=1))
+    for u in range(3):
+        joined = jnp.where(row < 6 - 2 * u, chunks[u], chunks[u + 1])
+        o_ref[pl.ds(16 * tile, 16), half, pl.ds(8 * u, 8)] = joined.astype(BF)
 
 
 def correlate_kernel(x_ref, o_ref, d_ref, m_ref, t_ref, f_ref, w_ref, qa_ref, qb_ref, l_ref):
@@ -178,7 +183,7 @@
         correlate_kernel,
         in_specs=[pl.BlockSpec(memory_space=pltpu.VMEM)],
         out_specs=pl.BlockSpec(memory_space=pltpu.VMEM),
-        out_shape=jax.ShapeDtypeStruct((64, 2, 4, BACK_ROWS, B), BF),
+        out_shape=jax.ShapeDtypeStruct((64, 2, 4 * BACK_ROWS, B), BF),
         scratch_shapes=[
             pltpu.VMEM((1280, 256), BF),
             pltpu.VMEM((1024, 256), BF),
@@ -213,8 +218,16 @@
     inner = row % B
     wanted = (inner // 8) * GSIZE + 4 * (row // B) + inner % 8
     spread = jnp.where((inner % 8 < 4) & (col == wanted), 1.0, 0.0).astype(BF)
+    tiles = [b_ref[:, pl.ds(8 * u, 8)].astype(F32) for u in range(3)]
+    line = lax.broadcasted_iota(jnp.int32, tiles[0].shape, 1)
+    chunks = [tiles[0]]
+    for t in range(1, parts):
+        part = jnp.roll(tiles[t - 1], 2 * t, axis=1)
+        if t < parts - 1:
+            part = jnp.where(line < 2 * t, part, jnp.roll(tiles[t], 2 * t, axis=1))
+        chunks.append(part)
     for t in range(parts):
-        chunk = b_ref[:, t].astype(F32).reshape(B * 8, B).astype(BF).T
+        chunk = chunks[t].reshape(B * 8, B).astype(BF).T
         for i in range(4):
             for b in range(steps):
                 l_ref[pl.ds((t * steps + b) * rows, rows), pl.ds(B * i, B)] = chunk[
@@ -233,8 +246,9 @@
             copy = send(d_ref.at[plane - 1, :, pl.ds(own * t, own)], plane, t)
             copy.start()
             copies.append(copy)
-    tail = b_ref[:, pl.ds(me_ref[0], 1)].reshape(b_ref.shape[0], 8, B).astype(F32)
-    line = lax.broadcasted_iota(jnp.int32, tail.shape, 1)
+    tail = chunks[0]
+    for t in range(1, parts):
+        tail = jnp.where(me_ref[0] == t, chunks[t], tail)
     h_ref[...] = jnp.sum(jnp.where((line == 4) | (line == 5), tail, 0.0), axis=1).T
     for copy in copies:
         copy.wait()
@@ -286,8 +300,8 @@
     home_q = swap(d_query.reshape(parts, rows, own), "tp")
     answer = correlate(signals.reshape(groups // 2, 2, OUT_ROWS, tokens))
     answer, home_q = lax.optimization_barrier((answer, home_q))
-    back = swap(answer.reshape(groups * parts, BACK_ROWS, tokens), ("ctx", "tp"))
-    back = back.reshape(groups, parts, BACK_ROWS, tokens)
+    back = swap(answer.reshape(groups * parts, BACK_ROWS // 2, 2, tokens), ("ctx", "tp"))
+    back = back.reshape(groups, parts * BACK_ROWS, tokens)
     d_saved, d_filters = finish(me, saved, home_q, back)
     return (d_saved.transpose(1, 0, 2), d_filters)
 

time: 158 us -> 153 us (0.968)
  blocking collectives: 100 us -> 94.3 us
    all_to_all x2, blocking collectives: 100 us -> 94.3 us  [swap(): return lax.all_to_all(x, axis, split_axis=0, concat_axis=0, tiled=True)]
where the time goes in v4:
time: 153 us; the launch traced here: 152 us
  blocking collectives  94.3 us (62%)
  Pallas kernels  20.6 us (13%)
  starting transfers between devices  20.6 us (13%)
  waiting for transfers between devices  14.6 us (10%)
    all_to_all x2, blocking collectives, swap(): return lax.all_to_all(x, axis, split_axis=0, concat_axis=0, tiled=True)  94.3 us
    pallas_call x1, Pallas kernels, correlate(): pl.pallas_call(correlate_kernel, in_specs=[pl.BlockSpec(memory_space=pltp...  16.8 us
    ppermute x3, waiting for transfers between devices, shift(): lax.ppermute(chunks[k], axis, [(i, (i + k) % size) for i in range(size)])  14.6 us
    ppermute x3, starting transfers between devices, shift(): lax.ppermute(chunks[k], axis, [(i, (i + k) % size) for i in range(size)])  13 us
    all_to_all x1, starting transfers between devices, swap(): return lax.all_to_all(x, axis, split_axis=0, concat_axis=0, tiled=True)  7.66 us
  transfers between devices with their start and end apart: 4, of which 2 were waited for; matrix products, arithmetic and copies ran while one was open for 0% of the time, Pallas kernels for 11%

profile of v4, /device:TPU:1, one launch (start us, length us, event | category | flops | bytes accessed | tf_op | source)
XLA Modules:
  0.0 152.5 jit_solution(4549386504267211388)
XLA Ops:
  0.6 0.0 copy-start
  0.6 1.4 copy-done
  2.0 0.0 copy-start.2
  2.0 0.0 copy-start.3
  2.0 0.0 copy-start.4
  2.1 0.1 shard_map.59
  2.2 5.0 %collective-permute-start = (bf16[2,32,2048]{2,1,0:T(8,128)(2,1)S(1)}, bf16[2,32,2048]{2,1,0:T(8,128)(2,1)S(1)}, u32[]{:S(2)}, u32[]{:S(2)}) collective-permute-start(bf16[2,32,2048]{2,1,0:T(8,128)(2,1)S(1)} %get-tuple-element.15), channel_id=1, source_target_pairs={{0,1},{1,2},{2,3},{3,0},{4,5},{5,6},{6,7},{7,4},{8,9},{9,10},{10,1... | collective-permute-start | bytes 786440 | tf_op jit(solution)/shard_map/ppermute | solution.py:285
  7.2 5.8 %collective-permute-start.1 = (bf16[2,32,2048]{2,1,0:T(8,128)(2,1)S(1)}, bf16[2,32,2048]{2,1,0:T(8,128)(2,1)S(1)}, u32[]{:S(2)}, u32[]{:S(2)}) collective-permute-start(bf16[2,32,2048]{2,1,0:T(8,128)(2,1)S(1)} %get-tuple-element.16), channel_id=1, source_target_pairs={{0,2},{1,3},{2,0},{3,1},{4,6},{5,7},{6,4},{7,5},{8,10},{9,11},{10,... | collective-permute-start | bytes 786440 | tf_op jit(solution)/shard_map/ppermute | solution.py:285
  13.0 2.2 %collective-permute-start.2 = (bf16[2,32,2048]{2,1,0:T(8,128)(2,1)S(1)}, bf16[2,32,2048]{2,1,0:T(8,128)(2,1)S(1)}, u32[]{:S(2)}, u32[]{:S(2)}) collective-permute-start(bf16[2,32,2048]{2,1,0:T(8,128)(2,1)S(1)} %get-tuple-element.17), channel_id=1, source_target_pairs={{0,3},{1,0},{2,1},{3,2},{4,7},{5,4},{6,5},{7,6},{8,11},{9,8},{10,9... | collective-permute-start | bytes 786440 | tf_op jit(solution)/shard_map/ppermute | solution.py:285
  15.2 0.0 collective-permute-done.refs_1_
  15.2 13.7 %collective-permute-done.1.refs_2_ = bf16[2,32,2048]{2,1,0:T(8,128)(2,1)S(1)} collective-permute-done((bf16[2,32,2048]{2,1,0:T(8,128)(2,1)S(1)}, bf16[2,32,2048]{2,1,0:T(8,128)(2,1)S(1)}, u32[]{:S(2)}, u32[]{:S(2)}) %collective-permute-start.1) | collective-permute-done | bytes 262176 | tf_op jit(solution)/shard_map/ppermute | solution.py:285
  28.8 1.0 collective-permute-done.2.refs_3_
  29.8 0.0 copy-done.2
  29.8 0.0 copy-done.3
  29.8 0.0 copy-done.4
  29.8 1.1 shard_map.60
  31.0 54.0 %all_to_all.15 = bf16[128,40,128]{2,1,0:T(8,128)(2,1)S(1)} all-to-all(bf16[128,40,128]{2,1,0:T(8,128)(2,1)S(1)} %get-tuple-element.18), channel_id=1, replica_groups=mesh['ctx'=128,'tp'=4] {'ctx'}, dimensions={0} | all-to-all | bytes 2621440 | tf_op jit(solution)/shard_map/all_to_all | solution.py:279
  85.0 7.7 %all-to-all-start.1 = ((bf16[4,32,2048]{2,1,0:T(8,128)(2,1)}), bf16[4,32,2048]{2,1,0:T(8,128)(2,1)S(1)}, u32[]{:S(2)}, u32[]{:S(2)}) async-start(bf16[4,32,2048]{2,1,0:T(8,128)(2,1)} %bitcast.3), calls=%async_computation.1 | async-start | bytes 1048576 | tf_op jit(solution)/shard_map/all_to_all | solution.py:279
  92.6 16.8 %shard_map.61 = bf16[64,2,24,128]{3,2,1,0:T(8,128)(2,1)S(1)} custom-call(bf16[64,2,40,128]{3,2,1,0:T(8,128)(2,1)S(1)} %bitcast.10), custom_call_target="tpu_custom_call" | custom-call | flops 21474836480 | bytes 67108864 | tf_op jit(solution)/shard_map/pallas_call | solution.py:182
  109.5 0.0 copy-start.1
  109.5 0.0 all-to-all-done.1.q_ref
  109.5 40.3 %all_to_all.16 = bf16[512,3,2,128]{3,2,1,0:T(2,128)(2,1)S(1)} all-to-all(bf16[512,3,2,128]{3,2,1,0:T(2,128)(2,1)S(1)} %bitcast.11), channel_id=1, replica_groups=mesh['ctx'=128,'tp'=4] {'ctx','tp'}, dimensions={0} | all-to-all | bytes 1572864 | tf_op jit(solution)/shard_map/all_to_all | solution.py:279
  149.8 0.0 copy-done.1
  149.8 2.5 %shard_map.62 = (bf16[3,32,8192]{2,1,0:T(8,128)(2,1)}, f32[128,128]{1,0:T(8,128)}) custom-call(s32[1]{0:T(128)} %bitcast.me_ref, bf16[3,32,8192]{2,1,0:T(8,128)(2,1)S(1)} %bitcast.8, bf16[4,32,2048]{2,1,0:T(8,128)(2,1)S(1)} %all-to-all-done.1.q_ref, bf16[128,24,128]{2,1,0:T(8,128)(2,1)S(1)} %bitcast.9), custom_call_target="tpu_custom_call" | custom-call | tf_op jit(solution)/shard_map/pallas_call | solution.py:261
Async XLA Ops:
  0.6 1.4 copy-start
  2.0 27.8 %copy-start.2 = (bf16[128,2048]{1,0:T(8,128)(2,1)S(1)}, bf16[128,2048]{1,0:T(8,128)(2,1)}, u32[]{:S(2)}) copy-start(bf16[128,2048]{1,0:T(8,128)(2,1)} %g_ref.1) | copy-start | bytes 1572868
  2.0 27.8 %copy-start.3 = (bf16[128,2048]{1,0:T(8,128)(2,1)S(1)}, bf16[128,2048]{1,0:T(8,128)(2,1)}, u32[]{:S(2)}) copy-start(bf16[128,2048]{1,0:T(8,128)(2,1)} %c_ref.1) | copy-start | bytes 1572868
  2.0 27.8 %copy-start.4 = (f32[128,128]{1,0:T(8,128)S(1)}, f32[128,128]{1,0:T(8,128)}, u32[]{:S(2)}) copy-start(f32[128,128]{1,0:T(8,128)} %h_ref.1) | copy-start | bytes 196612
  2.2 13.0 %collective-permute-start = (bf16[2,32,2048]{2,1,0:T(8,128)(2,1)S(1)}, bf16[2,32,2048]{2,1,0:T(8,128)(2,1)S(1)}, u32[]{:S(2)}, u32[]{:S(2)}) collective-permute-start(bf16[2,32,2048]{2,1,0:T(8,128)(2,1)S(1)} %get-tuple-element.15), channel_id=1, source_target_pairs={{0,1},{1,2},{2,3},{3,0},{4,5},{5,6},{6,7},{7,4},{8,9},{9,10},{10,1... | collective-permute-start | bytes 786440 | tf_op jit(solution)/shard_map/ppermute | solution.py:285
  7.2 21.7 %collective-permute-start.1 = (bf16[2,32,2048]{2,1,0:T(8,128)(2,1)S(1)}, bf16[2,32,2048]{2,1,0:T(8,128)(2,1)S(1)}, u32[]{:S(2)}, u32[]{:S(2)}) collective-permute-start(bf16[2,32,2048]{2,1,0:T(8,128)(2,1)S(1)} %get-tuple-element.16), channel_id=1, source_target_pairs={{0,2},{1,3},{2,0},{3,1},{4,6},{5,7},{6,4},{7,5},{8,10},{9,11},{10,... | collective-permute-start | bytes 786440 | tf_op jit(solution)/shard_map/ppermute | solution.py:285
  13.0 16.8 %collective-permute-start.2 = (bf16[2,32,2048]{2,1,0:T(8,128)(2,1)S(1)}, bf16[2,32,2048]{2,1,0:T(8,128)(2,1)S(1)}, u32[]{:S(2)}, u32[]{:S(2)}) collective-permute-start(bf16[2,32,2048]{2,1,0:T(8,128)(2,1)S(1)} %get-tuple-element.17), channel_id=1, source_target_pairs={{0,3},{1,0},{2,1},{3,2},{4,7},{5,4},{6,5},{7,6},{8,11},{9,8},{10,9... | collective-permute-start | bytes 786440 | tf_op jit(solution)/shard_map/ppermute | solution.py:285
  85.0 24.5 %all-to-all-start.1 = ((bf16[4,32,2048]{2,1,0:T(8,128)(2,1)}), bf16[4,32,2048]{2,1,0:T(8,128)(2,1)S(1)}, u32[]{:S(2)}, u32[]{:S(2)}) async-start(bf16[4,32,2048]{2,1,0:T(8,128)(2,1)} %bitcast.3), calls=%async_computation.1 | async-start | bytes 1048576 | tf_op jit(solution)/shard_map/all_to_all | solution.py:279
  109.5 40.3 %copy-start.1 = (bf16[32,3,8192]{2,0,1:T(8,128)(2,1)S(1)}, bf16[32,3,8192]{2,0,1:T(8,128)(2,1)}, u32[]{:S(2)}) copy-start(bf16[32,3,8192]{2,0,1:T(8,128)(2,1)} %param.4) | copy-start | bytes 4718596

commit v5 on v4

--- a/solution.py
+++ b/solution.py
@@ -7,71 +7,137 @@
 
 GSIZE = 16
 B = 128
-OUT_ROWS = 40
+OUT_ROWS = 10
 BACK_ROWS = 6
 F32 = jnp.float32
 BF = jnp.bfloat16
 
 
-def pack_rows_kernel(me_ref, s_ref, *o_refs):
-    parts = len(o_refs)
-    own = o_refs[0].shape[2]
-    for k, o_ref in enumerate(o_refs):
-        lanes = pl.ds(pl.multiple_of((me_ref[0] + k) % parts * own, own), own)
-        o_ref[0] = s_ref[0, :, lanes]
-        o_ref[1] = (s_ref[1, :, lanes].astype(F32) * s_ref[2, :, lanes].astype(F32)).astype(BF)
-
-
-def pack_rows(me, saved, parts):
-    _, rows, width = saved.shape
-    shape = jax.ShapeDtypeStruct((2, rows, width // parts), BF)
-    return pl.pallas_call(
-        pack_rows_kernel,
-        in_specs=[
-            pl.BlockSpec(memory_space=pltpu.SMEM),
-            pl.BlockSpec(memory_space=pltpu.VMEM),
-        ],
-        out_specs=[pl.BlockSpec(memory_space=pltpu.VMEM)] * parts,
-        out_shape=[shape] * parts,
-        compiler_params=pltpu.CompilerParams(vmem_limit_bytes=32 << 20),
-    )(me, saved)
-
-
-def pack_groups_kernel(me_ref, g_ref, c_ref, h_ref, *refs):
-    *a_refs, o_ref, q_ref, s_ref = refs
-    parts = len(a_refs)
-    tokens, span = g_ref.shape
-    rows = tokens // parts
-    count = span // GSIZE
-    grad = g_ref[...].astype(F32)
-    q_ref[...] = (grad * c_ref[...].astype(F32)).astype(BF)
-    for k, a_ref in enumerate(a_refs):
-        at = pl.multiple_of((me_ref[0] + parts - k) % parts * rows, rows)
-        s_ref[0, pl.ds(at, rows), :] = a_ref[0]
-        s_ref[1, pl.ds(at, rows), :] = a_ref[1]
-    delta = (s_ref[0].astype(F32) * grad).astype(BF)
-    o_ref[:, pl.ds(0, GSIZE), :] = delta.T.reshape(count, GSIZE, tokens)
-    o_ref[:, pl.ds(GSIZE, GSIZE), :] = s_ref[1].T.reshape(count, GSIZE, tokens)
-    taps = h_ref[...].T
-    o_ref[:, pl.ds(2 * GSIZE, 8), :] = jnp.broadcast_to(
-        taps[:, None, :], (count, 8, tokens)
-    ).astype(BF)
-
-
-def pack_groups(me, arrived, grad_out, conv_out, filters):
+def split_kernel(me_ref, g_ref, c_ref, *refs):
+    *g_refs, q_ref = refs
+    parts = len(g_refs)
+    rows = g_refs[0].shape[0]
+    for k, o_ref in enumerate(g_refs):
+        at = pl.multiple_of((me_ref[0] + k) % parts * rows, rows)
+        o_ref[...] = g_ref[pl.ds(at, rows), :]
+    q_ref[...] = (g_ref[...].astype(F32) * c_ref[...].astype(F32)).astype(BF)
+
+
+def split(me, grad_out, conv_out, parts):
     tokens, own = grad_out.shape
     vmem = pl.BlockSpec(memory_space=pltpu.VMEM)
+    chunk = jax.ShapeDtypeStruct((tokens // parts, own), BF)
     return pl.pallas_call(
-        pack_groups_kernel,
-        in_specs=[pl.BlockSpec(memory_space=pltpu.SMEM)] + [vmem] * (3 + len(arrived)),
-        out_specs=[vmem] * 2,
-        out_shape=(
-            jax.ShapeDtypeStruct((own // GSIZE, OUT_ROWS, tokens), BF),
-            jax.ShapeDtypeStruct((tokens, own), BF),
-        ),
-        scratch_shapes=[pltpu.VMEM((2, tokens, own), BF)],
+        split_kernel,
+        in_specs=[pl.BlockSpec(memory_space=pltpu.SMEM), vmem, vmem],
+        out_specs=[vmem] * (parts + 1),
+        out_shape=[chunk] * parts + [jax.ShapeDtypeStruct((tokens, own), BF)],
         compiler_params=pltpu.CompilerParams(vmem_limit_bytes=32 << 20),
-    )(me, grad_out, conv_out, filters, *arrived)
+    )(me, grad_out, conv_out)
+
+
+def pack_kernel(me_ref, s_ref, h_ref, *refs):
+    *g_refs, o_ref, f_ref, l_ref, c_ref = refs
+    parts = len(g_refs)
+    rows, own = g_refs[0].shape
+    steps = own // 256
+    span = steps * rows
+    for k, g_ref in enumerate(g_refs):
+        source = (me_ref[0] + parts - k) % parts
+        f_ref[pl.ds(pl.multiple_of(source * rows, rows), rows), :] = g_ref[...]
+    shape = (512, 512)
+    row = lax.broadcasted_iota(jnp.int32, shape, 0)
+    col = lax.broadcasted_iota(jnp.int32, shape, 1)
+    wanted = (row % 16) // 4 * B + (row % 256) // 16 * 8 + row // 256 * 4 + row % 4
+    gather = jnp.where(col == wanted, 1.0, 0.0).astype(BF)
+    for t in range(parts):
+        grad = f_ref[pl.ds(rows * t, rows), :].astype(F32)
+        lanes = pl.ds(own * t, own)
+        delta = (s_ref[0, :, lanes].astype(F32) * grad).astype(BF)
+        mixed = (s_ref[1, :, lanes].astype(F32) * s_ref[2, :, lanes].astype(F32)).astype(BF)
+        for b in range(steps):
+            at = pl.ds(b * rows, rows)
+            l_ref[at, pl.ds(0, 256)] = delta[:, 256 * b : 256 * b + 256]
+            l_ref[at, pl.ds(256, 256)] = mixed[:, 256 * b : 256 * b + 256]
+        spread = jnp.dot(l_ref[...], gather, preferred_element_type=F32)
+        for b in range(steps):
+            here = spread[b * rows : b * rows + rows]
+            block = jnp.concatenate([here[:, B * i : B * i + B] for i in range(4)], axis=0)
+            c_ref[t, pl.ds(16 * b, 16)] = block.T.reshape(16, 8, B)
+    taps = h_ref[...].T
+    shape = (16, 8, B)
+    line = lax.broadcasted_iota(jnp.int32, shape, 1)
+    for b in range(8):
+        groups = pl.ds(16 * b, 16)
+        filt = jnp.broadcast_to(taps[16 * b : 16 * b + 16][:, None], shape)
+        chunks = [c_ref[0, groups]] + [
+            jnp.roll(c_ref[t, groups], 2 * t, axis=1) for t in range(1, parts)
+        ]
+        for u in range(5):
+            tile = filt
+            if u < parts:
+                tile = jnp.where(line >= 2 * u, chunks[u], tile)
+            if u > 0:
+                tile = jnp.where(line < 2 * u - 2, chunks[u - 1], tile)
+            o_ref[groups, pl.ds(8 * u, 8)] = tile.astype(BF)
+
+
+def pack(me, saved, filters, grads):
+    parts = len(grads)
+    rows, own = grads[0].shape
+    vmem = pl.BlockSpec(memory_space=pltpu.VMEM)
+    return pl.pallas_call(
+        pack_kernel,
+        in_specs=[pl.BlockSpec(memory_space=pltpu.SMEM)] + [vmem] * (2 + parts),
+        out_specs=vmem,
+        out_shape=jax.ShapeDtypeStruct((own // GSIZE, parts * OUT_ROWS, B), BF),
+        scratch_shapes=[
+            pltpu.VMEM((parts * rows, own), BF),
+            pltpu.VMEM((own // 256 * rows, 512), BF),
+            pltpu.VMEM((parts, B, 8, B), F32),
+        ],
+        compiler_params=pltpu.CompilerParams(vmem_limit_bytes=32 << 20),
+    )(me, saved, filters, *grads)
+
+
+def ungroup(me, x_ref, d_ref, m_ref, n_ref):
+    shape = (16, 8, B)
+    line = lax.broadcasted_iota(jnp.int32, shape, 1)
+    lane = lax.broadcasted_iota(jnp.int32, shape, 2) // 32
+    for half in range(2):
+        lanes = pl.ds(B * half, B)
+        for b in range(4):
+            pairs = pl.ds(16 * b, 16)
+            tiles = [x_ref[pairs, half, pl.ds(8 * u, 8)].astype(F32) for u in range(5)]
+            chunks = [tiles[0]] + [
+                jnp.roll(jnp.where(line < 2 * t, tiles[t + 1], tiles[t]), 8 - 2 * t, axis=1)
+                for t in range(1, 4)
+            ]
+            taps = jnp.where((line == 6) | (line == 7), tiles[4], 0.0)
+            for t in range(3):
+                here = jnp.where((line == 2 * t) | (line == 2 * t + 1), tiles[t + 1], 0.0)
+                taps = jnp.where(me == t, here, taps)
+            taps = jnp.broadcast_to(0.5 * jnp.sum(taps, axis=1, keepdims=True), shape)
+            n_ref[pairs, half] = taps
+            turned = []
+            for d in range(4):
+                mix = chunks[(3 - d) % 4]
+                for i in range(3):
+                    mix = jnp.where(lane == i, chunks[(i - d) % 4], mix)
+                turned.append(mix if d == 0 else jnp.roll(mix, B - 32 * d, axis=2))
+            fours = []
+            for i in range(4):
+                mix = turned[(i - 3) % 4]
+                for t in range(3):
+                    mix = jnp.where(lane == t, turned[(i - t) % 4], mix)
+                fours.append(mix)
+            moved = [jnp.roll(x, 4, axis=1) for x in fours]
+            top = line < 4
+            delta = [jnp.where(top, fours[i], moved[i + 1]) for i in (0, 2)]
+            mixed = [jnp.where(top, moved[i], fours[i + 1]) for i in (0, 2)]
+            at = pl.ds(256 * b, 256)
+            d_ref[at, lanes] = jnp.concatenate(delta, axis=1).reshape(256, B).astype(BF)
+            m_ref[at, lanes] = jnp.concatenate(mixed, axis=1).reshape(256, B).astype(BF)
 
 
 def regroup(part, sums, o_ref, tile, half):
@@ -103,11 +169,10 @@
         o_ref[pl.ds(16 * tile, 16), half, pl.ds(8 * u, 8)] = joined.astype(BF)
 
 
-def correlate_kernel(x_ref, o_ref, d_ref, m_ref, t_ref, f_ref, w_ref, qa_ref, qb_ref, l_ref):
-    for half in range(2):
-        lanes = pl.ds(B * half, B)
-        d_ref[pl.ds(0, 1024), lanes] = x_ref[:, half, :GSIZE].reshape(1024, B)
-        m_ref[:, lanes] = x_ref[:, half, GSIZE : 2 * GSIZE].reshape(1024, B)
+def correlate_kernel(
+    me_ref, x_ref, o_ref, d_ref, m_ref, t_ref, f_ref, w_ref, qa_ref, qb_ref, l_ref, n_ref
+):
+    ungroup(me_ref[0], x_ref, d_ref, m_ref, n_ref)
     d_ref[pl.ds(1024, 256), :] = jnp.zeros((256, 256), BF)
     row = lax.broadcasted_iota(jnp.int32, (B, B), 0)
     col = lax.broadcasted_iota(jnp.int32, (B, B), 1)
@@ -151,7 +216,7 @@
 
     lax.fori_loop(0, 64, diagonals, 0, unroll=16)
     flip = jnp.where((row + col) % B == 0, 1.0, 0.0).astype(BF)
-    taps = x_ref[:, :, 2 * GSIZE :].astype(F32).reshape(1024, B).astype(BF)
+    taps = n_ref[...].reshape(1024, B).astype(BF)
     f_ref[...] = jnp.dot(taps, flip, preferred_element_type=F32).reshape(B, 8, B)
     lower = row >= col
     w_ref[pl.ds(0, B), pl.ds(B, B)] = jnp.zeros((B, B), BF)
@@ -178,10 +243,13 @@
             regroup(part, sums, o_ref, tile, half)
 
 
-def correlate(signals):
+def correlate(me, signals):
     return pl.pallas_call(
         correlate_kernel,
-        in_specs=[pl.BlockSpec(memory_space=pltpu.VMEM)],
+        in_specs=[
+            pl.BlockSpec(memory_space=pltpu.SMEM),
+            pl.BlockSpec(memory_space=pltpu.VMEM),
+        ],
         out_specs=pl.BlockSpec(memory_space=pltpu.VMEM),
         out_shape=jax.ShapeDtypeStruct((64, 2, 4 * BACK_ROWS, B), BF),
         scratch_shapes=[
@@ -193,12 +261,13 @@
             pltpu.VMEM((129, B, B), F32),
             pltpu.VMEM((65, B, B), F32),
             pltpu.VMEM((B, B), F32),
+            pltpu.VMEM((64, 2, 8, B), F32),
         ],
         compiler_params=pltpu.CompilerParams(vmem_limit_bytes=40 << 20),
         cost_estimate=pl.CostEstimate(
             flops=640 * 2 * 256**3, bytes_accessed=64 << 20, transcendentals=0
         ),
-    )(signals)
+    )(me, signals)
 
 
 def finish_kernel(me_ref, s_ref, q_ref, b_ref, o_ref, h_ref, l_ref, d_ref, sem):
@@ -294,11 +363,12 @@
     parts = width // own
     groups = own // GSIZE
     me = lax.axis_index("tp").reshape(1)
-    arrived = shift(pack_rows(me, saved, parts), "tp")
-    spread, d_query = pack_groups(me, arrived, grad_out, conv_out, filters)
-    signals, d_query = lax.optimization_barrier((swap(spread, "ctx"), d_query))
+    *grads, d_query = split(me, grad_out, conv_out, parts)
+    spread = pack(me, saved, filters, shift(grads, "tp"))
+    spread = spread.reshape(groups * parts, OUT_ROWS // 2, 2, tokens)
+    signals, d_query = lax.optimization_barrier((swap(spread, ("ctx", "tp")), d_query))
     home_q = swap(d_query.reshape(parts, rows, own), "tp")
-    answer = correlate(signals.reshape(groups // 2, 2, OUT_ROWS, tokens))
+    answer = correlate(me, signals.reshape(groups // 2, 2, parts * OUT_ROWS, tokens))
     answer, home_q = lax.optimization_barrier((answer, home_q))
     back = swap(answer.reshape(groups * parts, BACK_ROWS // 2, 2, tokens), ("ctx", "tp"))
     back = back.reshape(groups, parts * BACK_ROWS, tokens)

time: 153 us -> 149 us (0.974)
  waiting for transfers between devices: 14.6 us -> 5.55 us
  starting transfers between devices: 20.6 us -> 16.5 us
  Pallas kernels: 20.6 us -> 24 us
  blocking collectives: 94.3 us -> 97.5 us
  local copies, waits for them, and re-layouts: 1.42 us -> 4.33 us
    ppermute x3, waiting for transfers between devices: 14.6 us -> 5.54 us  [shift(): lax.ppermute(chunks[k], axis, [(i, (i + k) % size) for i in range(size)])]
    all_to_all x1, starting transfers between devices: 7.66 us -> 3.65 us  [swap(): return lax.all_to_all(x, axis, split_axis=0, concat_axis=0, tiled=True)]
    all_to_all x2, blocking collectives: 94.3 us -> 97.5 us  [swap(): return lax.all_to_all(x, axis, split_axis=0, concat_axis=0, tiled=True)]
    unnamed x10, local copies, waits for them, and re-layouts: 1.42 us -> 4.33 us
    pallas_call x1, Pallas kernels: 16.8 us -> 19.4 us  [correlate(): pl.pallas_call(correlate_kernel, in_specs=[pl.BlockSpec(memory_space=pltp...]
  transfers between devices with their start and end apart: 4 -> 4, of which waited for: 2 -> 1; matrix products, arithmetic and copies ran while one was open for 0% -> 0% of each run, Pallas kernels for 11% -> 13%
where the time goes in v5:
time: 149 us
  blocking collectives  97.5 us (65%)
  Pallas kernels  24 us (16%)
  starting transfers between devices  16.5 us (11%)
  waiting for transfers between devices  5.55 us (4%)
  local copies, waits for them, and re-layouts  4.33 us (3%)
    all_to_all x2, blocking collectives, swap(): return lax.all_to_all(x, axis, split_axis=0, concat_axis=0, tiled=True)  97.5 us
    pallas_call x1, Pallas kernels, correlate(): pl.pallas_call(correlate_kernel, in_specs=[pl.BlockSpec(memory_space=pltp...  19.4 us
    ppermute x3, starting transfers between devices, shift(): lax.ppermute(chunks[k], axis, [(i, (i + k) % size) for i in range(size)])  12.8 us
    ppermute x3, waiting for transfers between devices, shift(): lax.ppermute(chunks[k], axis, [(i, (i + k) % size) for i in range(size)])  5.54 us
    unnamed x10, local copies, waits for them, and re-layouts  4.33 us
    all_to_all x1, starting transfers between devices, swap(): return lax.all_to_all(x, axis, split_axis=0, concat_axis=0, tiled=True)  3.65 us
  transfers between devices with their start and end apart: 4, of which 1 were waited for; matrix products, arithmetic and copies ran while one was open for 0% of the time, Pallas kernels for 13%

profile of v5, /device:TPU:1, one launch (start us, length us, event | category | flops | bytes accessed | tf_op | source)
XLA Modules:
  0.0 148.8 jit_solution(5441843205777427101)
XLA Ops:
  0.6 0.0 copy-start.2
  0.6 1.0 copy-done.2
  1.7 0.0 copy-start.3
  1.7 1.0 copy-done.3
  2.7 0.9 shard_map.59
  3.6 4.8 %collective-permute-start = (bf16[32,2048]{1,0:T(8,128)(2,1)S(1)}, bf16[32,2048]{1,0:T(8,128)(2,1)S(1)}, u32[]{:S(2)}, u32[]{:S(2)}) collective-permute-start(bf16[32,2048]{1,0:T(8,128)(2,1)S(1)} %get-tuple-element.14), channel_id=1, source_target_pairs={{0,1},{1,2},{2,3},{3,0},{4,5},{5,6},{6,7},{7,4},{8,9},{9,10},{10,1... | collective-permute-start | bytes 393224 | tf_op jit(solution)/shard_map/ppermute | solution.py:354
  8.5 5.8 %collective-permute-start.1 = (bf16[32,2048]{1,0:T(8,128)(2,1)S(1)}, bf16[32,2048]{1,0:T(8,128)(2,1)S(1)}, u32[]{:S(2)}, u32[]{:S(2)}) collective-permute-start(bf16[32,2048]{1,0:T(8,128)(2,1)S(1)} %get-tuple-element.15), channel_id=1, source_target_pairs={{0,2},{1,3},{2,0},{3,1},{4,6},{5,7},{6,4},{7,5},{8,10},{9,11},{10,... | collective-permute-start | bytes 393224 | tf_op jit(solution)/shard_map/ppermute | solution.py:354
  14.3 2.2 %collective-permute-start.2 = (bf16[32,2048]{1,0:T(8,128)(2,1)S(1)}, bf16[32,2048]{1,0:T(8,128)(2,1)S(1)}, u32[]{:S(2)}, u32[]{:S(2)}) collective-permute-start(bf16[32,2048]{1,0:T(8,128)(2,1)S(1)} %get-tuple-element.16), channel_id=1, source_target_pairs={{0,3},{1,0},{2,1},{3,2},{4,7},{5,4},{6,5},{7,6},{8,11},{9,8},{10,9... | collective-permute-start | bytes 393224 | tf_op jit(solution)/shard_map/ppermute | solution.py:354
  16.5 0.0 collective-permute-done.refs_1_
  16.5 5.5 %collective-permute-done.1.refs_2_ = bf16[32,2048]{1,0:T(8,128)(2,1)S(1)} collective-permute-done((bf16[32,2048]{1,0:T(8,128)(2,1)S(1)}, bf16[32,2048]{1,0:T(8,128)(2,1)S(1)}, u32[]{:S(2)}, u32[]{:S(2)}) %collective-permute-start.1) | collective-permute-done | bytes 131104 | tf_op jit(solution)/shard_map/ppermute | solution.py:354
  22.0 0.0 collective-permute-done.2.refs_3_
  22.0 0.0 copy-start
  22.0 1.4 copy-done
  23.4 0.0 copy-start.4
  23.4 0.8 copy-done.4
  24.3 1.2 shard_map.60
  25.5 59.3 %all_to_all.15 = bf16[512,5,2,128]{3,2,1,0:T(2,128)(2,1)S(1)} all-to-all(bf16[512,5,2,128]{3,2,1,0:T(2,128)(2,1)S(1)} %bitcast.10), channel_id=1, replica_groups=mesh['ctx'=128,'tp'=4] {'ctx','tp'}, dimensions={0} | all-to-all | bytes 2621440 | tf_op jit(solution)/shard_map/all_to_all | solution.py:348
  84.8 3.7 %all-to-all-start.1 = ((bf16[4,32,2048]{2,1,0:T(8,128)(2,1)}), bf16[4,32,2048]{2,1,0:T(8,128)(2,1)S(1)}, u32[]{:S(2)}, u32[]{:S(2)}) async-start(bf16[4,32,2048]{2,1,0:T(8,128)(2,1)} %bitcast.4), calls=%async_computation.1 | async-start | bytes 1048576 | tf_op jit(solution)/shard_map/all_to_all | solution.py:348
  88.5 19.4 %shard_map.61 = bf16[64,2,24,128]{3,2,1,0:T(8,128)(2,1)S(1)} custom-call(s32[1]{0:T(128)} %bitcast.me_ref, bf16[64,2,40,128]{3,2,1,0:T(8,128)(2,1)S(1)} %bitcast.12), custom_call_target="tpu_custom_call" | custom-call | flops 21474836480 | bytes 67108864 | tf_op jit(solution)/shard_map/pallas_call | solution.py:247
  107.9 0.0 copy-start.1
  107.9 0.0 all-to-all-done.1.q_ref
  107.9 38.2 %all_to_all.16 = bf16[512,3,2,128]{3,2,1,0:T(2,128)(2,1)S(1)} all-to-all(bf16[512,3,2,128]{3,2,1,0:T(2,128)(2,1)S(1)} %bitcast.13), channel_id=1, replica_groups=mesh['ctx'=128,'tp'=4] {'ctx','tp'}, dimensions={0} | all-to-all | bytes 1572864 | tf_op jit(solution)/shard_map/all_to_all | solution.py:348
  146.2 0.0 copy-done.1
  146.2 2.5 %shard_map.62 = (bf16[3,32,8192]{2,1,0:T(8,128)(2,1)}, f32[128,128]{1,0:T(8,128)}) custom-call(s32[1]{0:T(128)} %bitcast.me_ref, bf16[3,32,8192]{2,1,0:T(8,128)(2,1)S(1)} %bitcast.9, bf16[4,32,2048]{2,1,0:T(8,128)(2,1)S(1)} %all-to-all-done.1.q_ref, bf16[128,24,128]{2,1,0:T(8,128)(2,1)S(1)} %bitcast.11), custom_call_target="tpu_custom_call" | custom-call | tf_op jit(solution)/shard_map/pallas_call | solution.py:330
Async XLA Ops:
  0.6 1.0 copy-start.2
  1.7 1.0 copy-start.3
  3.6 12.8 %collective-permute-start = (bf16[32,2048]{1,0:T(8,128)(2,1)S(1)}, bf16[32,2048]{1,0:T(8,128)(2,1)S(1)}, u32[]{:S(2)}, u32[]{:S(2)}) collective-permute-start(bf16[32,2048]{1,0:T(8,128)(2,1)S(1)} %get-tuple-element.14), channel_id=1, source_target_pairs={{0,1},{1,2},{2,3},{3,0},{4,5},{5,6},{6,7},{7,4},{8,9},{9,10},{10,1... | collective-permute-start | bytes 393224 | tf_op jit(solution)/shard_map/ppermute | solution.py:354
  8.5 13.6 %collective-permute-start.1 = (bf16[32,2048]{1,0:T(8,128)(2,1)S(1)}, bf16[32,2048]{1,0:T(8,128)(2,1)S(1)}, u32[]{:S(2)}, u32[]{:S(2)}) collective-permute-start(bf16[32,2048]{1,0:T(8,128)(2,1)S(1)} %get-tuple-element.15), channel_id=1, source_target_pairs={{0,2},{1,3},{2,0},{3,1},{4,6},{5,7},{6,4},{7,5},{8,10},{9,11},{10,... | collective-permute-start | bytes 393224 | tf_op jit(solution)/shard_map/ppermute | solution.py:354
  14.3 7.7 %collective-permute-start.2 = (bf16[32,2048]{1,0:T(8,128)(2,1)S(1)}, bf16[32,2048]{1,0:T(8,128)(2,1)S(1)}, u32[]{:S(2)}, u32[]{:S(2)}) collective-permute-start(bf16[32,2048]{1,0:T(8,128)(2,1)S(1)} %get-tuple-element.16), channel_id=1, source_target_pairs={{0,3},{1,0},{2,1},{3,2},{4,7},{5,4},{6,5},{7,6},{8,11},{9,8},{10,9... | collective-permute-start | bytes 393224 | tf_op jit(solution)/shard_map/ppermute | solution.py:354
  22.0 1.4 copy-start
  23.4 0.8 copy-start.4
  84.8 23.1 %all-to-all-start.1 = ((bf16[4,32,2048]{2,1,0:T(8,128)(2,1)}), bf16[4,32,2048]{2,1,0:T(8,128)(2,1)S(1)}, u32[]{:S(2)}, u32[]{:S(2)}) async-start(bf16[4,32,2048]{2,1,0:T(8,128)(2,1)} %bitcast.4), calls=%async_computation.1 | async-start | bytes 1048576 | tf_op jit(solution)/shard_map/all_to_all | solution.py:348
  107.9 38.3 %copy-start.1 = (bf16[32,3,8192]{2,0,1:T(8,128)(2,1)S(1)}, bf16[32,3,8192]{2,0,1:T(8,128)(2,1)}, u32[]{:S(2)}) copy-start(bf16[32,3,8192]{2,0,1:T(8,128)(2,1)} %param.4) | copy-start | bytes 4718596

commit v6 on v5

--- a/solution.py
+++ b/solution.py
@@ -13,63 +13,114 @@
 BF = jnp.bfloat16
 
 
-def split_kernel(me_ref, g_ref, c_ref, *refs):
-    *g_refs, q_ref = refs
+def split_kernel(me_ref, g_ref, *refs):
+    *g_refs, sem = refs
     parts = len(g_refs)
     rows = g_refs[0].shape[0]
+    copies = []
     for k, o_ref in enumerate(g_refs):
         at = pl.multiple_of((me_ref[0] + k) % parts * rows, rows)
-        o_ref[...] = g_ref[pl.ds(at, rows), :]
-    q_ref[...] = (g_ref[...].astype(F32) * c_ref[...].astype(F32)).astype(BF)
-
-
-def split(me, grad_out, conv_out, parts):
+        copies.append(pltpu.make_async_copy(g_ref.at[pl.ds(at, rows), :], o_ref, sem.at[k]))
+    for copy in copies:
+        copy.start()
+    for copy in copies:
+        copy.wait()
+
+
+def split(me, grad_out, parts):
     tokens, own = grad_out.shape
     vmem = pl.BlockSpec(memory_space=pltpu.VMEM)
     chunk = jax.ShapeDtypeStruct((tokens // parts, own), BF)
     return pl.pallas_call(
         split_kernel,
-        in_specs=[pl.BlockSpec(memory_space=pltpu.SMEM), vmem, vmem],
-        out_specs=[vmem] * (parts + 1),
-        out_shape=[chunk] * parts + [jax.ShapeDtypeStruct((tokens, own), BF)],
+        in_specs=[
+            pl.BlockSpec(memory_space=pltpu.SMEM),
+            pl.BlockSpec(memory_space=pl.ANY),
+        ],
+        out_specs=[vmem] * parts,
+        out_shape=[chunk] * parts,
+        scratch_shapes=[pltpu.SemaphoreType.DMA((parts,))],
+        compiler_params=pltpu.CompilerParams(vmem_limit_bytes=16 << 20),
+    )(me, grad_out)
+
+
+def gather(values, offset, l_ref, store):
+    rows, own = values.shape
+    steps = own // 256
+    shape = (256, 512)
+    row = lax.broadcasted_iota(jnp.int32, shape, 0)
+    col = lax.broadcasted_iota(jnp.int32, shape, 1)
+    wanted = (row % 16) // 4 * B + row // 16 * 8 + offset + row % 4
+    weights = jnp.where(col == wanted, 1.0, 0.0).astype(BF)
+    for b in range(steps):
+        l_ref[pl.ds(b * rows, rows), :] = values[:, 256 * b : 256 * b + 256]
+    spread = jnp.dot(l_ref[...], weights, preferred_element_type=F32)
+    for b in range(steps):
+        here = spread[b * rows : b * rows + rows]
+        block = jnp.concatenate([here[:, B * i : B * i + B] for i in range(4)], axis=0)
+        store(b, block.T.reshape(16, 8, B))
+
+
+def prepare_kernel(after_ref, s_ref, g_ref, c_ref, h_ref, q_ref, m_ref, d_ref, t_ref, l_ref):
+    del after_ref
+    parts = m_ref.shape[0]
+    own = g_ref.shape[1]
+    q_ref[...] = s_ref[0]
+    d_ref[...] = (g_ref[...].astype(F32) * c_ref[...].astype(F32)).astype(BF)
+    t_ref[...] = h_ref[...].T
+    for t in range(parts):
+        lanes = pl.ds(own * t, own)
+        mixed = (s_ref[1, :, lanes].astype(F32) * s_ref[2, :, lanes].astype(F32)).astype(BF)
+
+        def store(b, block):
+            m_ref[t, pl.ds(16 * b, 16)] = block
+
+        gather(mixed, 4, l_ref, store)
+
+
+def prepare(after, saved, grad_out, conv_out, filters, parts):
+    _, rows, width = saved.shape
+    tokens, own = grad_out.shape
+    vmem = pl.BlockSpec(memory_space=pltpu.VMEM)
+    return pl.pallas_call(
+        prepare_kernel,
+        in_specs=[pl.BlockSpec(memory_space=pltpu.SMEM)] + [vmem] * 4,
+        out_specs=[vmem] * 4,
+        out_shape=(
+            jax.ShapeDtypeStruct((rows, width), BF),
+            jax.ShapeDtypeStruct((parts, B, 8, B), F32),
+            jax.ShapeDtypeStruct((tokens, own), BF),
+            jax.ShapeDtypeStruct((own // GSIZE, tokens), F32),
+        ),
+        scratch_shapes=[pltpu.VMEM((own // 256 * rows, 256), BF)],
         compiler_params=pltpu.CompilerParams(vmem_limit_bytes=32 << 20),
-    )(me, grad_out, conv_out)
-
-
-def pack_kernel(me_ref, s_ref, h_ref, *refs):
+        cost_estimate=pl.CostEstimate(
+            flops=2 << 30, bytes_accessed=8 << 20, transcendentals=0
+        ),
+    )(after, saved, grad_out, conv_out, filters)
+
+
+def pack_kernel(me_ref, s_ref, m_ref, t_ref, *refs):
     *g_refs, o_ref, f_ref, l_ref, c_ref = refs
     parts = len(g_refs)
     rows, own = g_refs[0].shape
-    steps = own // 256
-    span = steps * rows
     for k, g_ref in enumerate(g_refs):
         source = (me_ref[0] + parts - k) % parts
         f_ref[pl.ds(pl.multiple_of(source * rows, rows), rows), :] = g_ref[...]
-    shape = (512, 512)
-    row = lax.broadcasted_iota(jnp.int32, shape, 0)
-    col = lax.broadcasted_iota(jnp.int32, shape, 1)
-    wanted = (row % 16) // 4 * B + (row % 256) // 16 * 8 + row // 256 * 4 + row % 4
-    gather = jnp.where(col == wanted, 1.0, 0.0).astype(BF)
     for t in range(parts):
         grad = f_ref[pl.ds(rows * t, rows), :].astype(F32)
-        lanes = pl.ds(own * t, own)
-        delta = (s_ref[0, :, lanes].astype(F32) * grad).astype(BF)
-        mixed = (s_ref[1, :, lanes].astype(F32) * s_ref[2, :, lanes].astype(F32)).astype(BF)
-        for b in range(steps):
-            at = pl.ds(b * rows, rows)
-            l_ref[at, pl.ds(0, 256)] = delta[:, 256 * b : 256 * b + 256]
-            l_ref[at, pl.ds(256, 256)] = mixed[:, 256 * b : 256 * b + 256]
-        spread = jnp.dot(l_ref[...], gather, preferred_element_type=F32)
-        for b in range(steps):
-            here = spread[b * rows : b * rows + rows]
-            block = jnp.concatenate([here[:, B * i : B * i + B] for i in range(4)], axis=0)
-            c_ref[t, pl.ds(16 * b, 16)] = block.T.reshape(16, 8, B)
-    taps = h_ref[...].T
+        delta = (s_ref[:, pl.ds(own * t, own)].astype(F32) * grad).astype(BF)
+
+        def store(b, block):
+            groups = pl.ds(16 * b, 16)
+            c_ref[t, groups] = block + m_ref[t, groups]
+
+        gather(delta, 0, l_ref, store)
     shape = (16, 8, B)
     line = lax.broadcasted_iota(jnp.int32, shape, 1)
     for b in range(8):
         groups = pl.ds(16 * b, 16)
-        filt = jnp.broadcast_to(taps[16 * b : 16 * b + 16][:, None], shape)
+        filt = jnp.broadcast_to(t_ref[groups, :][:, None], shape)
         chunks = [c_ref[0, groups]] + [
             jnp.roll(c_ref[t, groups], 2 * t, axis=1) for t in range(1, parts)
         ]
@@ -82,22 +133,22 @@
             o_ref[groups, pl.ds(8 * u, 8)] = tile.astype(BF)
 
 
-def pack(me, saved, filters, grads):
+def pack(me, query, mixed, taps, grads):
     parts = len(grads)
     rows, own = grads[0].shape
     vmem = pl.BlockSpec(memory_space=pltpu.VMEM)
     return pl.pallas_call(
         pack_kernel,
-        in_specs=[pl.BlockSpec(memory_space=pltpu.SMEM)] + [vmem] * (2 + parts),
+        in_specs=[pl.BlockSpec(memory_space=pltpu.SMEM)] + [vmem] * (3 + parts),
         out_specs=vmem,
         out_shape=jax.ShapeDtypeStruct((own // GSIZE, parts * OUT_ROWS, B), BF),
         scratch_shapes=[
             pltpu.VMEM((parts * rows, own), BF),
-            pltpu.VMEM((own // 256 * rows, 512), BF),
+            pltpu.VMEM((own // 256 * rows, 256), BF),
             pltpu.VMEM((parts, B, 8, B), F32),
         ],
         compiler_params=pltpu.CompilerParams(vmem_limit_bytes=32 << 20),
-    )(me, saved, filters, *grads)
+    )(me, query, mixed, taps, *grads)
 
 
 def ungroup(me, x_ref, d_ref, m_ref, n_ref):
@@ -177,6 +228,22 @@
     row = lax.broadcasted_iota(jnp.int32, (B, B), 0)
     col = lax.broadcasted_iota(jnp.int32, (B, B), 1)
 
+    flip = jnp.where((row + col) % B == 0, 1.0, 0.0).astype(BF)
+    taps = n_ref[...].reshape(1024, B).astype(BF)
+    f_ref[...] = jnp.dot(taps, flip, preferred_element_type=F32).reshape(B, 8, B)
+    lower = row >= col
+    w_ref[pl.ds(0, B), pl.ds(B, B)] = jnp.zeros((B, B), BF)
+
+    def build(e, before):
+        line = jnp.broadcast_to(f_ref[pl.ds(e, 1)], (16, 8, B)).reshape(B, B)
+        turned = pltpu.roll(line, 0, 1, stride=1, stride_axis=0)
+        block = jnp.where(lower, turned, before).astype(BF)
+        at = pl.multiple_of(e * B, B)
+        w_ref[pl.ds(at, B), pl.ds(0, B)] = block
+        w_ref[pl.ds(at + B, B), pl.ds(B, B)] = block
+        return turned
+
+    before = jnp.zeros((B, B), F32)
     mirror = jnp.where(row + col == B - 1, 1.0, 0.0).astype(BF)
     for half in range(2):
         t_ref[pl.ds(B * half, B), :] = lax.dot_general(
@@ -198,9 +265,9 @@
             qa_ref[2 * e] = table[:B, :B] + table[B:, B:]
             qa_ref[2 * e + 1] = table[:B, B:]
             qb_ref[e] = table[B:, :B]
-            return carry
-
-        lax.fori_loop(0, 16, gram, 0, unroll=16)
+            return build(2 * e + 1, build(2 * e, carry))
+
+        before = lax.fori_loop(0, 16, gram, before, unroll=16)
     qb_ref[64] = jnp.zeros((B, B), F32)
     qa_ref[128] = jnp.zeros((B, B), F32)
     keep = row + col >= B - 1
@@ -214,29 +281,14 @@
             l_ref[pl.ds(2 * e + u, 1), :] = jnp.sum(turned, axis=0, keepdims=True)
         return carry
 
-    lax.fori_loop(0, 64, diagonals, 0, unroll=16)
-    flip = jnp.where((row + col) % B == 0, 1.0, 0.0).astype(BF)
-    taps = n_ref[...].reshape(1024, B).astype(BF)
-    f_ref[...] = jnp.dot(taps, flip, preferred_element_type=F32).reshape(B, 8, B)
-    lower = row >= col
-    w_ref[pl.ds(0, B), pl.ds(B, B)] = jnp.zeros((B, B), BF)
-
-    def build(e, before):
-        line = jnp.broadcast_to(f_ref[pl.ds(e, 1)], (16, 8, B)).reshape(B, B)
-        turned = pltpu.roll(line, 0, 1, stride=1, stride_axis=0)
-        block = jnp.where(lower, turned, before).astype(BF)
-        at = pl.multiple_of(e * B, B)
-        w_ref[pl.ds(at, B), pl.ds(0, B)] = block
-        w_ref[pl.ds(at + B, B), pl.ds(B, B)] = block
-        return turned
-
-    lax.fori_loop(0, B, build, jnp.zeros((B, B), F32), unroll=16)
     for tile in range(4):
         count = 64 - 16 * tile
         left = jnp.concatenate(
             [d_ref[pl.ds(256 * tile + 16 * u, 256), :] for u in range(count)], axis=1
         )
         total = jnp.dot(left, w_ref[pl.ds(0, 256 * count), :], preferred_element_type=F32)
+        for e in range(16 * tile, 16 * tile + 16):
+            diagonals(e, 0)
         for half in range(2):
             part = total[:, B * half : B * half + B].reshape(16, GSIZE, B)
             sums = l_ref[pl.ds(32 * tile + half, 16, stride=2), :]
@@ -363,8 +415,9 @@
     parts = width // own
     groups = own // GSIZE
     me = lax.axis_index("tp").reshape(1)
-    *grads, d_query = split(me, grad_out, conv_out, parts)
-    spread = pack(me, saved, filters, shift(grads, "tp"))
+    *grads, after = lax.optimization_barrier((*split(me, grad_out, parts), me))
+    query, mixed, d_query, taps = prepare(after, saved, grad_out, conv_out, filters, parts)
+    spread = pack(me, query, mixed, taps, shift(grads, "tp"))
     spread = spread.reshape(groups * parts, OUT_ROWS // 2, 2, tokens)
     signals, d_query = lax.optimization_barrier((swap(spread, ("ctx", "tp")), d_query))
     home_q = swap(d_query.reshape(parts, rows, own), "tp")

time: 149 us -> 142 us (0.953)
  waiting for transfers between devices: 5.55 us -> 0.01 us
  Pallas kernels: 24 us -> 21 us
    ppermute x3, waiting for transfers between devices: 5.54 us -> 0.01 us  [shift(): lax.ppermute(chunks[k], axis, [(i, (i + k) % size) for i in range(size)])]
    pallas_call x1, Pallas kernels: 19.4 us -> 14.8 us  [correlate(): pl.pallas_call(correlate_kernel, in_specs=[pl.BlockSpec(memory_space=pltp...]
    pallas_call x0 -> x1, Pallas kernels: none -> 1.95 us  [prepare(): pl.pallas_call(prepare_kernel, in_specs=[pl.BlockSpec(memory_space=pltpu....]
    unnamed x10 -> x12, local copies, waits for them, and re-layouts: 4.33 us -> 5.37 us
  transfers between devices with their start and end apart: 4 -> 4, of which waited for: 1 -> 0; matrix products, arithmetic and copies ran while one was open for 0% -> 0% of each run, Pallas kernels for 13% -> 12%
where the time goes in v6:
time: 142 us; the launch traced here: 141 us
  blocking collectives  97.4 us (69%)
  Pallas kernels  21 us (15%)
  starting transfers between devices  16.5 us (12%)
  local copies, waits for them, and re-layouts  5.37 us (4%)
    all_to_all x2, blocking collectives, swap(): return lax.all_to_all(x, axis, split_axis=0, concat_axis=0, tiled=True)  97.4 us
    pallas_call x1, Pallas kernels, correlate(): pl.pallas_call(correlate_kernel, in_specs=[pl.BlockSpec(memory_space=pltp...  14.8 us
    ppermute x3, starting transfers between devices, shift(): lax.ppermute(chunks[k], axis, [(i, (i + k) % size) for i in range(size)])  12.8 us
    unnamed x12, local copies, waits for them, and re-layouts  5.37 us
    all_to_all x1, starting transfers between devices, swap(): return lax.all_to_all(x, axis, split_axis=0, concat_axis=0, tiled=True)  3.65 us
  transfers between devices with their start and end apart: 4, of which 0 were waited for; matrix products, arithmetic and copies ran while one was open for 0% of the time, Pallas kernels for 12%

profile of v6, /device:TPU:1, one launch (start us, length us, event | category | flops | bytes accessed | tf_op | source)
XLA Modules:
  0.0 141.2 jit_solution(10943671098738909321)
XLA Ops:
  0.6 0.0 copy-start.2
  0.6 1.0 copy-done.2
  1.7 0.7 shard_map.59
  2.4 4.8 %collective-permute-start = (bf16[32,2048]{1,0:T(8,128)(2,1)S(1)}, bf16[32,2048]{1,0:T(8,128)(2,1)S(1)}, u32[]{:S(2)}, u32[]{:S(2)}) collective-permute-start(bf16[32,2048]{1,0:T(8,128)(2,1)S(1)} %get-tuple-element.30), channel_id=1, source_target_pairs={{0,1},{1,2},{2,3},{3,0},{4,5},{5,6},{6,7},{7,4},{8,9},{9,10},{10,1... | collective-permute-start | bytes 393224 | tf_op jit(solution)/shard_map/ppermute | solution.py:406
  7.2 5.8 %collective-permute-start.1 = (bf16[32,2048]{1,0:T(8,128)(2,1)S(1)}, bf16[32,2048]{1,0:T(8,128)(2,1)S(1)}, u32[]{:S(2)}, u32[]{:S(2)}) collective-permute-start(bf16[32,2048]{1,0:T(8,128)(2,1)S(1)} %get-tuple-element.31), channel_id=1, source_target_pairs={{0,2},{1,3},{2,0},{3,1},{4,6},{5,7},{6,4},{7,5},{8,10},{9,11},{10,... | collective-permute-start | bytes 393224 | tf_op jit(solution)/shard_map/ppermute | solution.py:406
  13.0 2.2 %collective-permute-start.2 = (bf16[32,2048]{1,0:T(8,128)(2,1)S(1)}, bf16[32,2048]{1,0:T(8,128)(2,1)S(1)}, u32[]{:S(2)}, u32[]{:S(2)}) collective-permute-start(bf16[32,2048]{1,0:T(8,128)(2,1)S(1)} %get-tuple-element.32), channel_id=1, source_target_pairs={{0,3},{1,0},{2,1},{3,2},{4,7},{5,4},{6,5},{7,6},{8,11},{9,8},{10,9... | collective-permute-start | bytes 393224 | tf_op jit(solution)/shard_map/ppermute | solution.py:406
  15.2 0.0 copy-start
  15.2 1.4 copy-done
  16.6 1.0 copy-done.3
  17.7 1.0 copy-done.4
  18.7 0.8 copy-done.5
  19.5 2.0 %shard_map.60 = (bf16[32,8192]{1,0:T(8,128)(2,1)S(1)}, f32[4,128,8,128]{3,2,1,0:T(8,128)S(1)}, bf16[128,2048]{1,0:T(8,128)(2,1)}, f32[128,128]{1,0:T(8,128)S(1)}) custom-call(s32[1]{0:T(128)} %bitcast.me_ref.after_ref, bf16[3,32,8192]{2,1,0:T(8,128)(2,1)S(1)} %bitcast.10, bf16[128,2048]{1,0:T(8,128)(2,1)S(1)} %copy-done.3, bf16[128,2048]{1,0:T(8,128)(2,1)S(1)} %copy-done.4, ...), custom_call_target="tpu_custom_call" | custom-call | flops 2147483648 | bytes 8388608 | tf_op jit(solution)/shard_map/pallas_call | solution.py:85
  21.5 0.0 collective-permute-done.refs_1_
  21.5 0.0 collective-permute-done.1.refs_2_
  21.5 0.0 collective-permute-done.2.refs_3_
  21.5 1.0 shard_map.61
  22.6 59.2 %all_to_all.15 = bf16[512,5,2,128]{3,2,1,0:T(2,128)(2,1)S(1)} all-to-all(bf16[512,5,2,128]{3,2,1,0:T(2,128)(2,1)S(1)} %bitcast.8), channel_id=1, replica_groups=mesh['ctx'=128,'tp'=4] {'ctx','tp'}, dimensions={0} | all-to-all | bytes 2621440 | tf_op jit(solution)/shard_map/all_to_all | solution.py:400
  81.7 3.7 %all-to-all-start.1 = ((bf16[4,32,2048]{2,1,0:T(8,128)(2,1)}), bf16[4,32,2048]{2,1,0:T(8,128)(2,1)S(1)}, u32[]{:S(2)}, u32[]{:S(2)}) async-start(bf16[4,32,2048]{2,1,0:T(8,128)(2,1)} %bitcast.4), calls=%async_computation.1 | async-start | bytes 1048576 | tf_op jit(solution)/shard_map/all_to_all | solution.py:400
  85.4 14.8 %shard_map.62 = bf16[64,2,24,128]{3,2,1,0:T(8,128)(2,1)S(1)} custom-call(s32[1]{0:T(128)} %bitcast.me_ref.after_ref, bf16[64,2,40,128]{3,2,1,0:T(8,128)(2,1)S(1)} %bitcast.12), custom_call_target="tpu_custom_call" | custom-call | flops 21474836480 | bytes 67108864 | tf_op jit(solution)/shard_map/pallas_call | solution.py:299
  100.2 0.0 copy-start.1
  100.2 0.0 all-to-all-done.1.q_ref
  100.2 38.2 %all_to_all.16 = bf16[512,3,2,128]{3,2,1,0:T(2,128)(2,1)S(1)} all-to-all(bf16[512,3,2,128]{3,2,1,0:T(2,128)(2,1)S(1)} %bitcast.13), channel_id=1, replica_groups=mesh['ctx'=128,'tp'=4] {'ctx','tp'}, dimensions={0} | all-to-all | bytes 1572864 | tf_op jit(solution)/shard_map/all_to_all | solution.py:400
  138.5 0.0 copy-done.1
  138.5 2.5 %shard_map.63 = (bf16[3,32,8192]{2,1,0:T(8,128)(2,1)}, f32[128,128]{1,0:T(8,128)}) custom-call(s32[1]{0:T(128)} %bitcast.me_ref.after_ref, bf16[3,32,8192]{2,1,0:T(8,128)(2,1)S(1)} %bitcast.11, bf16[4,32,2048]{2,1,0:T(8,128)(2,1)S(1)} %all-to-all-done.1.q_ref, bf16[128,24,128]{2,1,0:T(8,128)(2,1)S(1)} %bitcast.9), custom_call_target="tpu_custom_call" | custom-call | tf_op jit(solution)/shard_map/pallas_call | solution.py:382
  (3 shorter events, 0.0 us)
Async XLA Ops:
  0.6 1.0 copy-start.2
  2.4 19.1 %collective-permute-start = (bf16[32,2048]{1,0:T(8,128)(2,1)S(1)}, bf16[32,2048]{1,0:T(8,128)(2,1)S(1)}, u32[]{:S(2)}, u32[]{:S(2)}) collective-permute-start(bf16[32,2048]{1,0:T(8,128)(2,1)S(1)} %get-tuple-element.30), channel_id=1, source_target_pairs={{0,1},{1,2},{2,3},{3,0},{4,5},{5,6},{6,7},{7,4},{8,9},{9,10},{10,1... | collective-permute-start | bytes 393224 | tf_op jit(solution)/shard_map/ppermute | solution.py:406
  7.2 14.3 %collective-permute-start.1 = (bf16[32,2048]{1,0:T(8,128)(2,1)S(1)}, bf16[32,2048]{1,0:T(8,128)(2,1)S(1)}, u32[]{:S(2)}, u32[]{:S(2)}) collective-permute-start(bf16[32,2048]{1,0:T(8,128)(2,1)S(1)} %get-tuple-element.31), channel_id=1, source_target_pairs={{0,2},{1,3},{2,0},{3,1},{4,6},{5,7},{6,4},{7,5},{8,10},{9,11},{10,... | collective-permute-start | bytes 393224 | tf_op jit(solution)/shard_map/ppermute | solution.py:406
  13.0 8.5 %collective-permute-start.2 = (bf16[32,2048]{1,0:T(8,128)(2,1)S(1)}, bf16[32,2048]{1,0:T(8,128)(2,1)S(1)}, u32[]{:S(2)}, u32[]{:S(2)}) collective-permute-start(bf16[32,2048]{1,0:T(8,128)(2,1)S(1)} %get-tuple-element.32), channel_id=1, source_target_pairs={{0,3},{1,0},{2,1},{3,2},{4,7},{5,4},{6,5},{7,6},{8,11},{9,8},{10,9... | collective-permute-start | bytes 393224 | tf_op jit(solution)/shard_map/ppermute | solution.py:406
  15.2 1.4 copy-start
  16.6 1.0 copy-start.3
  17.7 1.0 copy-start.4
  18.7 0.8 copy-start.5
  81.7 18.5 %all-to-all-start.1 = ((bf16[4,32,2048]{2,1,0:T(8,128)(2,1)}), bf16[4,32,2048]{2,1,0:T(8,128)(2,1)S(1)}, u32[]{:S(2)}, u32[]{:S(2)}) async-start(bf16[4,32,2048]{2,1,0:T(8,128)(2,1)} %bitcast.4), calls=%async_computation.1 | async-start | bytes 1048576 | tf_op jit(solution)/shard_map/all_to_all | solution.py:400
  100.2 38.3 %copy-start.1 = (bf16[32,3,8192]{2,0,1:T(8,128)(2,1)S(1)}, bf16[32,3,8192]{2,0,1:T(8,128)(2,1)}, u32[]{:S(2)}) copy-start(bf16[32,3,8192]{2,0,1:T(8,128)(2,1)} %param.4) | copy-start | bytes 4718596

commit v7 on v6

--- a/solution.py
+++ b/solution.py
@@ -3,12 +3,15 @@
 from jax import lax
 from jax.experimental import pallas as pl
 from jax.experimental.pallas import tpu as pltpu
+from jax.sharding import Mesh
 from jax.sharding import PartitionSpec as P
 
 GSIZE = 16
 B = 128
 OUT_ROWS = 10
 BACK_ROWS = 6
+CTX = {"y": 8, "zh": 2, "x": 4, "core": 2}
+ORDER = ("x", "core", "y", "zh", "tp")
 F32 = jnp.float32
 BF = jnp.bfloat16
 
@@ -130,7 +133,10 @@
                 tile = jnp.where(line >= 2 * u, chunks[u], tile)
             if u > 0:
                 tile = jnp.where(line < 2 * u - 2, chunks[u - 1], tile)
-            o_ref[groups, pl.ds(8 * u, 8)] = tile.astype(BF)
+            tile = tile.astype(BF).reshape(2, 4, 2, 8, B)
+            for x in range(4):
+                for core in range(2):
+                    o_ref[x, core, b, :, pl.ds(8 * u, 8)] = tile[:, x, core]
 
 
 def pack(me, query, mixed, taps, grads):
@@ -141,7 +147,7 @@
         pack_kernel,
         in_specs=[pl.BlockSpec(memory_space=pltpu.SMEM)] + [vmem] * (3 + parts),
         out_specs=vmem,
-        out_shape=jax.ShapeDtypeStruct((own // GSIZE, parts * OUT_ROWS, B), BF),
+        out_shape=jax.ShapeDtypeStruct((4, 2, 8, 2, parts * OUT_ROWS, B), BF),
         scratch_shapes=[
             pltpu.VMEM((parts * rows, own), BF),
             pltpu.VMEM((own // 256 * rows, 256), BF),
@@ -159,7 +165,14 @@
         lanes = pl.ds(B * half, B)
         for b in range(4):
             pairs = pl.ds(16 * b, 16)
-            tiles = [x_ref[pairs, half, pl.ds(8 * u, 8)].astype(F32) for u in range(5)]
+            tiles = [
+                jnp.stack(
+                    [x_ref[x, half, pl.ds(2 * b, 2), :, pl.ds(8 * u, 8)] for x in range(4)], axis=2
+                )
+                .reshape(shape)
+                .astype(F32)
+                for u in range(5)
+            ]
             chunks = [tiles[0]] + [
                 jnp.roll(jnp.where(line < 2 * t, tiles[t + 1], tiles[t]), 8 - 2 * t, axis=1)
                 for t in range(1, 4)
@@ -217,7 +230,9 @@
         chunks.append(chunk if t == 0 else jnp.roll(chunk, 8 - 2 * t, axis=1))
     for u in range(3):
         joined = jnp.where(row < 6 - 2 * u, chunks[u], chunks[u + 1])
-        o_ref[pl.ds(16 * tile, 16), half, pl.ds(8 * u, 8)] = joined.astype(BF)
+        joined = joined.astype(BF).reshape(2, 2, 4, 8, B)
+        for x in range(4):
+            o_ref[x, half, pl.ds(2 * tile, 2), :, pl.ds(8 * u, 8)] = joined[:, :, x]
 
 
 def correlate_kernel(
@@ -303,7 +318,7 @@
             pl.BlockSpec(memory_space=pltpu.VMEM),
         ],
         out_specs=pl.BlockSpec(memory_space=pltpu.VMEM),
-        out_shape=jax.ShapeDtypeStruct((64, 2, 4 * BACK_ROWS, B), BF),
+        out_shape=jax.ShapeDtypeStruct((4, 2, 8, 2, 4 * BACK_ROWS, B), BF),
         scratch_shapes=[
             pltpu.VMEM((1280, 256), BF),
             pltpu.VMEM((1024, 256), BF),
@@ -339,7 +354,18 @@
     inner = row % B
     wanted = (inner // 8) * GSIZE + 4 * (row // B) + inner % 8
     spread = jnp.where((inner % 8 < 4) & (col == wanted), 1.0, 0.0).astype(BF)
-    tiles = [b_ref[:, pl.ds(8 * u, 8)].astype(F32) for u in range(3)]
+    tiles = [
+        jnp.stack(
+            [
+                jnp.stack([b_ref[x, core, :, :, pl.ds(8 * u, 8)] for core in range(2)], axis=2)
+                for x in range(4)
+            ],
+            axis=2,
+        )
+        .reshape(B, 8, B)
+        .astype(F32)
+        for u in range(3)
+    ]
     line = lax.broadcasted_iota(jnp.int32, tiles[0].shape, 1)
     chunks = [tiles[0]]
     for t in range(1, parts):
@@ -419,22 +445,25 @@
     query, mixed, d_query, taps = prepare(after, saved, grad_out, conv_out, filters, parts)
     spread = pack(me, query, mixed, taps, shift(grads, "tp"))
     spread = spread.reshape(groups * parts, OUT_ROWS // 2, 2, tokens)
-    signals, d_query = lax.optimization_barrier((swap(spread, ("ctx", "tp")), d_query))
+    signals, d_query = lax.optimization_barrier((swap(spread, ORDER), d_query))
     home_q = swap(d_query.reshape(parts, rows, own), "tp")
-    answer = correlate(me, signals.reshape(groups // 2, 2, parts * OUT_ROWS, tokens))
+    answer = correlate(me, signals.reshape(4, 2, 8, 2, parts * OUT_ROWS, tokens))
     answer, home_q = lax.optimization_barrier((answer, home_q))
-    back = swap(answer.reshape(groups * parts, BACK_ROWS // 2, 2, tokens), ("ctx", "tp"))
-    back = back.reshape(groups, parts * BACK_ROWS, tokens)
+    back = swap(answer.reshape(groups * parts, BACK_ROWS // 2, 2, tokens), ORDER)
+    back = back.reshape(4, 2, 8, 2, parts * BACK_ROWS, tokens)
     d_saved, d_filters = finish(me, saved, home_q, back)
     return (d_saved.transpose(1, 0, 2), d_filters)
 
 
 def solution(mesh):
-    placed = (P(("ctx", "tp"), None, None), P("ctx", "tp"), P("ctx", "tp"), P("ctx", "tp"))
+    names = tuple(CTX) + ("tp",)
+    split_mesh = Mesh(mesh.devices.reshape(*CTX.values(), -1), names)
+    ctx = tuple(CTX)
+    placed = (P(names, None, None), P(ctx, "tp"), P(ctx, "tp"), P(ctx, "tp"))
     return jax.shard_map(
         per_device,
-        mesh=mesh,
+        mesh=split_mesh,
         in_specs=placed,
-        out_specs=(P(("ctx", "tp"), None, None), P("ctx", "tp")),
+        out_specs=(P(names, None, None), P(ctx, "tp")),
         check_vma=False,
     )

time: 142 us -> 142 us (level)
  no operation moved by 1% of the time
where the time goes in v7:
time: 142 us; the launch traced here: 141 us
  blocking collectives  97.6 us (69%)
  Pallas kernels  21 us (15%)
  starting transfers between devices  16.5 us (12%)
  local copies, waits for them, and re-layouts  5.37 us (4%)
    all_to_all x2, blocking collectives, swap(): return lax.all_to_all(x, axis, split_axis=0, concat_axis=0, tiled=True)  97.6 us
    pallas_call x1, Pallas kernels, correlate(): pl.pallas_call(correlate_kernel, in_specs=[pl.BlockSpec(memory_space=pltp...  14.8 us
    ppermute x3, starting transfers between devices, shift(): lax.ppermute(chunks[k], axis, [(i, (i + k) % size) for i in range(size)])  12.8 us
    unnamed x12, local copies, waits for them, and re-layouts  5.37 us
    all_to_all x1, starting transfers between devices, swap(): return lax.all_to_all(x, axis, split_axis=0, concat_axis=0, tiled=True)  3.65 us
  transfers between devices with their start and end apart: 4, of which 0 were waited for; matrix products, arithmetic and copies ran while one was open for 0% of the time, Pallas kernels for 12%

profile of v7, /device:TPU:1, one launch (start us, length us, event | category | flops | bytes accessed | tf_op | source)
XLA Modules:
  0.0 141.3 jit_solution(11983300114345979305)
XLA Ops:
  0.6 0.0 copy-start.2
  0.6 1.0 copy-done.2
  1.7 0.7 shard_map.59
  2.4 4.8 %collective-permute-start = (bf16[32,2048]{1,0:T(8,128)(2,1)S(1)}, bf16[32,2048]{1,0:T(8,128)(2,1)S(1)}, u32[]{:S(2)}, u32[]{:S(2)}) collective-permute-start(bf16[32,2048]{1,0:T(8,128)(2,1)S(1)} %get-tuple-element.30), channel_id=1, source_target_pairs={{0,1},{1,2},{2,3},{3,0},{4,5},{5,6},{6,7},{7,4},{8,9},{9,10},{10,1... | collective-permute-start | bytes 393224 | tf_op jit(solution)/shard_map/ppermute | solution.py:432
  7.2 5.8 %collective-permute-start.1 = (bf16[32,2048]{1,0:T(8,128)(2,1)S(1)}, bf16[32,2048]{1,0:T(8,128)(2,1)S(1)}, u32[]{:S(2)}, u32[]{:S(2)}) collective-permute-start(bf16[32,2048]{1,0:T(8,128)(2,1)S(1)} %get-tuple-element.31), channel_id=1, source_target_pairs={{0,2},{1,3},{2,0},{3,1},{4,6},{5,7},{6,4},{7,5},{8,10},{9,11},{10,... | collective-permute-start | bytes 393224 | tf_op jit(solution)/shard_map/ppermute | solution.py:432
  13.0 2.2 %collective-permute-start.2 = (bf16[32,2048]{1,0:T(8,128)(2,1)S(1)}, bf16[32,2048]{1,0:T(8,128)(2,1)S(1)}, u32[]{:S(2)}, u32[]{:S(2)}) collective-permute-start(bf16[32,2048]{1,0:T(8,128)(2,1)S(1)} %get-tuple-element.32), channel_id=1, source_target_pairs={{0,3},{1,0},{2,1},{3,2},{4,7},{5,4},{6,5},{7,6},{8,11},{9,8},{10,9... | collective-permute-start | bytes 393224 | tf_op jit(solution)/shard_map/ppermute | solution.py:432
  15.2 0.0 copy-start
  15.2 1.4 copy-done
  16.6 1.0 copy-done.3
  17.7 1.0 copy-done.4
  18.7 0.8 copy-done.5
  19.5 2.0 %shard_map.60 = (bf16[32,8192]{1,0:T(8,128)(2,1)S(1)}, f32[4,128,8,128]{3,2,1,0:T(8,128)S(1)}, bf16[128,2048]{1,0:T(8,128)(2,1)}, f32[128,128]{1,0:T(8,128)S(1)}) custom-call(s32[1]{0:T(128)} %bitcast.me_ref.after_ref, bf16[3,32,8192]{2,1,0:T(8,128)(2,1)S(1)} %bitcast.10, bf16[128,2048]{1,0:T(8,128)(2,1)S(1)} %copy-done.3, bf16[128,2048]{1,0:T(8,128)(2,1)S(1)} %copy-done.4, ...), custom_call_target="tpu_custom_call" | custom-call | flops 2147483648 | bytes 8388608 | tf_op jit(solution)/shard_map/pallas_call | solution.py:88
  21.5 0.0 collective-permute-done.refs_1_
  21.5 0.0 collective-permute-done.1.refs_2_
  21.5 0.0 collective-permute-done.2.refs_3_
  21.5 1.0 shard_map.61
  22.6 59.9 %all_to_all.15 = bf16[512,5,2,128]{3,2,1,0:T(2,128)(2,1)S(1)} all-to-all(bf16[512,5,2,128]{3,2,1,0:T(2,128)(2,1)S(1)} %bitcast.8), channel_id=1, replica_groups=mesh['y'=8,'zh'=2,'x'=4,'core'=2,'tp'=4] {'x','core','y','zh','tp'}, dimensions={0} | all-to-all | bytes 2621440 | tf_op jit(solution)/shard_map/all_to_all | solution.py:426
  82.4 3.7 %all-to-all-start.1 = ((bf16[4,32,2048]{2,1,0:T(8,128)(2,1)}), bf16[4,32,2048]{2,1,0:T(8,128)(2,1)S(1)}, u32[]{:S(2)}, u32[]{:S(2)}) async-start(bf16[4,32,2048]{2,1,0:T(8,128)(2,1)} %bitcast.4), calls=%async_computation.1 | async-start | bytes 1048576 | tf_op jit(solution)/shard_map/all_to_all | solution.py:426
  86.1 14.8 %shard_map.62 = bf16[4,2,8,2,24,128]{5,4,3,2,1,0:T(8,128)(2,1)S(1)} custom-call(s32[1]{0:T(128)} %bitcast.me_ref.after_ref, bf16[4,2,8,2,40,128]{5,4,3,2,1,0:T(8,128)(2,1)S(1)} %bitcast.12), custom_call_target="tpu_custom_call" | custom-call | flops 21474836480 | bytes 67108864 | tf_op jit(solution)/shard_map/pallas_call | solution.py:314
  101.0 0.0 copy-start.1
  101.0 0.0 all-to-all-done.1.q_ref
  101.0 37.7 %all_to_all.16 = bf16[512,3,2,128]{3,2,1,0:T(2,128)(2,1)S(1)} all-to-all(bf16[512,3,2,128]{3,2,1,0:T(2,128)(2,1)S(1)} %bitcast.13), channel_id=1, replica_groups=mesh['y'=8,'zh'=2,'x'=4,'core'=2,'tp'=4] {'x','core','y','zh','tp'}, dimensions={0} | all-to-all | bytes 1572864 | tf_op jit(solution)/shard_map/all_to_all | solution.py:426
  138.6 0.0 copy-done.1
  138.6 2.5 %shard_map.63 = (bf16[3,32,8192]{2,1,0:T(8,128)(2,1)}, f32[128,128]{1,0:T(8,128)}) custom-call(s32[1]{0:T(128)} %bitcast.me_ref.after_ref, bf16[3,32,8192]{2,1,0:T(8,128)(2,1)S(1)} %bitcast.11, bf16[4,32,2048]{2,1,0:T(8,128)(2,1)S(1)} %all-to-all-done.1.q_ref, bf16[4,2,8,2,24,128]{5,4,3,2,1,0:T(8,128)(2,1)S(1)} %bitcast.9), custom_call_target="tpu_custom_call" | custom-call | tf_op jit(solution)/shard_map/pallas_call | solution.py:408
  (3 shorter events, 0.0 us)
Async XLA Ops:
  0.6 1.0 copy-start.2
  2.4 19.1 %collective-permute-start = (bf16[32,2048]{1,0:T(8,128)(2,1)S(1)}, bf16[32,2048]{1,0:T(8,128)(2,1)S(1)}, u32[]{:S(2)}, u32[]{:S(2)}) collective-permute-start(bf16[32,2048]{1,0:T(8,128)(2,1)S(1)} %get-tuple-element.30), channel_id=1, source_target_pairs={{0,1},{1,2},{2,3},{3,0},{4,5},{5,6},{6,7},{7,4},{8,9},{9,10},{10,1... | collective-permute-start | bytes 393224 | tf_op jit(solution)/shard_map/ppermute | solution.py:432
  7.2 14.3 %collective-permute-start.1 = (bf16[32,2048]{1,0:T(8,128)(2,1)S(1)}, bf16[32,2048]{1,0:T(8,128)(2,1)S(1)}, u32[]{:S(2)}, u32[]{:S(2)}) collective-permute-start(bf16[32,2048]{1,0:T(8,128)(2,1)S(1)} %get-tuple-element.31), channel_id=1, source_target_pairs={{0,2},{1,3},{2,0},{3,1},{4,6},{5,7},{6,4},{7,5},{8,10},{9,11},{10,... | collective-permute-start | bytes 393224 | tf_op jit(solution)/shard_map/ppermute | solution.py:432
  13.0 8.5 %collective-permute-start.2 = (bf16[32,2048]{1,0:T(8,128)(2,1)S(1)}, bf16[32,2048]{1,0:T(8,128)(2,1)S(1)}, u32[]{:S(2)}, u32[]{:S(2)}) collective-permute-start(bf16[32,2048]{1,0:T(8,128)(2,1)S(1)} %get-tuple-element.32), channel_id=1, source_target_pairs={{0,3},{1,0},{2,1},{3,2},{4,7},{5,4},{6,5},{7,6},{8,11},{9,8},{10,9... | collective-permute-start | bytes 393224 | tf_op jit(solution)/shard_map/ppermute | solution.py:432
  15.2 1.4 copy-start
  16.6 1.0 copy-start.3
  17.7 1.0 copy-start.4
  18.7 0.8 copy-start.5
  82.4 18.5 %all-to-all-start.1 = ((bf16[4,32,2048]{2,1,0:T(8,128)(2,1)}), bf16[4,32,2048]{2,1,0:T(8,128)(2,1)S(1)}, u32[]{:S(2)}, u32[]{:S(2)}) async-start(bf16[4,32,2048]{2,1,0:T(8,128)(2,1)} %bitcast.4), calls=%async_computation.1 | async-start | bytes 1048576 | tf_op jit(solution)/shard_map/all_to_all | solution.py:426
  101.0 37.7 %copy-start.1 = (bf16[32,3,8192]{2,0,1:T(8,128)(2,1)S(1)}, bf16[32,3,8192]{2,0,1:T(8,128)(2,1)}, u32[]{:S(2)}) copy-start(bf16[32,3,8192]{2,0,1:T(8,128)(2,1)} %param.4) | copy-start | bytes 4718596

commit v8 on v6

--- a/solution.py
+++ b/solution.py
@@ -11,37 +11,6 @@
 BACK_ROWS = 6
 F32 = jnp.float32
 BF = jnp.bfloat16
-
-
-def split_kernel(me_ref, g_ref, *refs):
-    *g_refs, sem = refs
-    parts = len(g_refs)
-    rows = g_refs[0].shape[0]
-    copies = []
-    for k, o_ref in enumerate(g_refs):
-        at = pl.multiple_of((me_ref[0] + k) % parts * rows, rows)
-        copies.append(pltpu.make_async_copy(g_ref.at[pl.ds(at, rows), :], o_ref, sem.at[k]))
-    for copy in copies:
-        copy.start()
-    for copy in copies:
-        copy.wait()
-
-
-def split(me, grad_out, parts):
-    tokens, own = grad_out.shape
-    vmem = pl.BlockSpec(memory_space=pltpu.VMEM)
-    chunk = jax.ShapeDtypeStruct((tokens // parts, own), BF)
-    return pl.pallas_call(
-        split_kernel,
-        in_specs=[
-            pl.BlockSpec(memory_space=pltpu.SMEM),
-            pl.BlockSpec(memory_space=pl.ANY),
-        ],
-        out_specs=[vmem] * parts,
-        out_shape=[chunk] * parts,
-        scratch_shapes=[pltpu.SemaphoreType.DMA((parts,))],
-        compiler_params=pltpu.CompilerParams(vmem_limit_bytes=16 << 20),
-    )(me, grad_out)
 
 
 def gather(values, offset, l_ref, store):
@@ -415,7 +384,12 @@
     parts = width // own
     groups = own // GSIZE
     me = lax.axis_index("tp").reshape(1)
-    *grads, after = lax.optimization_barrier((*split(me, grad_out, parts), me))
+    own_rows = grad_out.reshape(parts, rows, own)
+    grads = [
+        lax.dynamic_index_in_dim(own_rows, lax.rem(me[0] + k, parts), 0, keepdims=False)
+        for k in range(parts)
+    ]
+    *grads, after = lax.optimization_barrier((*grads, me))
     query, mixed, d_query, taps = prepare(after, saved, grad_out, conv_out, filters, parts)
     spread = pack(me, query, mixed, taps, shift(grads, "tp"))
     spread = spread.reshape(groups * parts, OUT_ROWS // 2, 2, tokens)

time: 142 us -> 141 us (level)
    unnamed x12 -> x10, local copies, waits for them, and re-layouts: 5.37 us -> 4.33 us
where the time goes in v8:
time: 141 us
  blocking collectives  97.4 us (69%)
  Pallas kernels  20.3 us (14%)
  starting transfers between devices  16.5 us (12%)
  local copies, waits for them, and re-layouts  5.47 us (4%)
    all_to_all x2, blocking collectives, swap(): return lax.all_to_all(x, axis, split_axis=0, concat_axis=0, tiled=True)  97.4 us
    pallas_call x1, Pallas kernels, correlate(): pl.pallas_call(correlate_kernel, in_specs=[pl.BlockSpec(memory_space=pltp...  14.8 us
    ppermute x3, starting transfers between devices, shift(): lax.ppermute(chunks[k], axis, [(i, (i + k) % size) for i in range(size)])  12.8 us
    unnamed x10, local copies, waits for them, and re-layouts  4.33 us
    all_to_all x1, starting transfers between devices, swap(): return lax.all_to_all(x, axis, split_axis=0, concat_axis=0, tiled=True)  3.65 us
  transfers between devices with their start and end apart: 4, of which 0 were waited for; matrix products, arithmetic and copies ran while one was open for 0% of the time, Pallas kernels for 12%

profile of v8, /device:TPU:1, one launch (start us, length us, event | category | flops | bytes accessed | tf_op | source)
XLA Modules:
  0.0 140.6 jit_solution(12622228378062325282)
XLA Ops:
  0.7 1.1 dynamic-slice_bitcast_fusion
  1.8 4.8 %collective-permute-start = (bf16[32,2048]{1,0:T(8,128)(2,1)S(1)}, bf16[32,2048]{1,0:T(8,128)(2,1)S(1)}, u32[]{:S(2)}, u32[]{:S(2)}) collective-permute-start(bf16[32,2048]{1,0:T(8,128)(2,1)S(1)} %get-tuple-element.22), channel_id=1, source_target_pairs={{0,1},{1,2},{2,3},{3,0},{4,5},{5,6},{6,7},{7,4},{8,9},{9,10},{10,1... | collective-permute-start | bytes 393224 | tf_op jit(solution)/shard_map/ppermute | solution.py:375
  6.6 5.8 %collective-permute-start.1 = (bf16[32,2048]{1,0:T(8,128)(2,1)S(1)}, bf16[32,2048]{1,0:T(8,128)(2,1)S(1)}, u32[]{:S(2)}, u32[]{:S(2)}) collective-permute-start(bf16[32,2048]{1,0:T(8,128)(2,1)S(1)} %get-tuple-element.23), channel_id=1, source_target_pairs={{0,2},{1,3},{2,0},{3,1},{4,6},{5,7},{6,4},{7,5},{8,10},{9,11},{10,... | collective-permute-start | bytes 393224 | tf_op jit(solution)/shard_map/ppermute | solution.py:375
  12.5 2.2 %collective-permute-start.2 = (bf16[32,2048]{1,0:T(8,128)(2,1)S(1)}, bf16[32,2048]{1,0:T(8,128)(2,1)S(1)}, u32[]{:S(2)}, u32[]{:S(2)}) collective-permute-start(bf16[32,2048]{1,0:T(8,128)(2,1)S(1)} %get-tuple-element.24), channel_id=1, source_target_pairs={{0,3},{1,0},{2,1},{3,2},{4,7},{5,4},{6,5},{7,6},{8,11},{9,8},{10,9... | collective-permute-start | bytes 393224 | tf_op jit(solution)/shard_map/ppermute | solution.py:375
  14.6 0.0 copy-start
  14.7 1.4 copy-done
  16.1 0.0 copy-start.2
  16.1 1.0 copy-done.2
  17.1 0.0 copy-start.3
  17.1 1.0 copy-done.3
  18.1 0.8 copy-done.4
  19.0 2.0 %shard_map.59 = (bf16[32,8192]{1,0:T(8,128)(2,1)S(1)}, f32[4,128,8,128]{3,2,1,0:T(8,128)S(1)}, bf16[128,2048]{1,0:T(8,128)(2,1)}, f32[128,128]{1,0:T(8,128)S(1)}) custom-call(s32[1]{0:T(128)} %bitcast.after_ref.me_ref, bf16[3,32,8192]{2,1,0:T(8,128)(2,1)S(1)} %bitcast.19, bf16[128,2048]{1,0:T(8,128)(2,1)S(1)} %copy-done.2, bf16[128,2048]{1,0:T(8,128)(2,1)S(1)} %copy-done.3, ...), custom_call_target="tpu_custom_call" | custom-call | flops 2147483648 | bytes 8388608 | tf_op jit(solution)/shard_map/pallas_call | solution.py:54
  20.9 0.0 collective-permute-done.refs_1_
  20.9 0.0 collective-permute-done.1.refs_2_
  20.9 0.0 collective-permute-done.2.refs_3_
  21.0 1.0 shard_map.60
  22.0 59.2 %all_to_all.15 = bf16[512,5,2,128]{3,2,1,0:T(2,128)(2,1)S(1)} all-to-all(bf16[512,5,2,128]{3,2,1,0:T(2,128)(2,1)S(1)} %bitcast.17), channel_id=1, replica_groups=mesh['ctx'=128,'tp'=4] {'ctx','tp'}, dimensions={0} | all-to-all | bytes 2621440 | tf_op jit(solution)/shard_map/all_to_all | solution.py:369
  81.2 3.7 %all-to-all-start.1 = ((bf16[4,32,2048]{2,1,0:T(8,128)(2,1)}), bf16[4,32,2048]{2,1,0:T(8,128)(2,1)S(1)}, u32[]{:S(2)}, u32[]{:S(2)}) async-start(bf16[4,32,2048]{2,1,0:T(8,128)(2,1)} %bitcast.9), calls=%async_computation.1 | async-start | bytes 1048576 | tf_op jit(solution)/shard_map/all_to_all | solution.py:369
  84.8 14.8 %shard_map.61 = bf16[64,2,24,128]{3,2,1,0:T(8,128)(2,1)S(1)} custom-call(s32[1]{0:T(128)} %bitcast.after_ref.me_ref, bf16[64,2,40,128]{3,2,1,0:T(8,128)(2,1)S(1)} %bitcast.21), custom_call_target="tpu_custom_call" | custom-call | flops 21474836480 | bytes 67108864 | tf_op jit(solution)/shard_map/pallas_call | solution.py:268
  99.7 0.0 copy-start.1
  99.7 0.0 all-to-all-done.1.q_ref
  99.7 38.2 %all_to_all.16 = bf16[512,3,2,128]{3,2,1,0:T(2,128)(2,1)S(1)} all-to-all(bf16[512,3,2,128]{3,2,1,0:T(2,128)(2,1)S(1)} %bitcast.22), channel_id=1, replica_groups=mesh['ctx'=128,'tp'=4] {'ctx','tp'}, dimensions={0} | all-to-all | bytes 1572864 | tf_op jit(solution)/shard_map/all_to_all | solution.py:369
  137.9 0.0 copy-done.1
  137.9 2.5 %shard_map.62 = (bf16[3,32,8192]{2,1,0:T(8,128)(2,1)}, f32[128,128]{1,0:T(8,128)}) custom-call(s32[1]{0:T(128)} %bitcast.after_ref.me_ref, bf16[3,32,8192]{2,1,0:T(8,128)(2,1)S(1)} %bitcast.20, bf16[4,32,2048]{2,1,0:T(8,128)(2,1)S(1)} %all-to-all-done.1.q_ref, bf16[128,24,128]{2,1,0:T(8,128)(2,1)S(1)} %bitcast.18), custom_call_target="tpu_custom_call" | custom-call | tf_op jit(solution)/shard_map/pallas_call | solution.py:351
  (1 shorter events, 0.0 us)
Async XLA Ops:
  1.8 19.1 %collective-permute-start = (bf16[32,2048]{1,0:T(8,128)(2,1)S(1)}, bf16[32,2048]{1,0:T(8,128)(2,1)S(1)}, u32[]{:S(2)}, u32[]{:S(2)}) collective-permute-start(bf16[32,2048]{1,0:T(8,128)(2,1)S(1)} %get-tuple-element.22), channel_id=1, source_target_pairs={{0,1},{1,2},{2,3},{3,0},{4,5},{5,6},{6,7},{7,4},{8,9},{9,10},{10,1... | collective-permute-start | bytes 393224 | tf_op jit(solution)/shard_map/ppermute | solution.py:375
  6.6 14.3 %collective-permute-start.1 = (bf16[32,2048]{1,0:T(8,128)(2,1)S(1)}, bf16[32,2048]{1,0:T(8,128)(2,1)S(1)}, u32[]{:S(2)}, u32[]{:S(2)}) collective-permute-start(bf16[32,2048]{1,0:T(8,128)(2,1)S(1)} %get-tuple-element.23), channel_id=1, source_target_pairs={{0,2},{1,3},{2,0},{3,1},{4,6},{5,7},{6,4},{7,5},{8,10},{9,11},{10,... | collective-permute-start | bytes 393224 | tf_op jit(solution)/shard_map/ppermute | solution.py:375
  12.5 8.5 %collective-permute-start.2 = (bf16[32,2048]{1,0:T(8,128)(2,1)S(1)}, bf16[32,2048]{1,0:T(8,128)(2,1)S(1)}, u32[]{:S(2)}, u32[]{:S(2)}) collective-permute-start(bf16[32,2048]{1,0:T(8,128)(2,1)S(1)} %get-tuple-element.24), channel_id=1, source_target_pairs={{0,3},{1,0},{2,1},{3,2},{4,7},{5,4},{6,5},{7,6},{8,11},{9,8},{10,9... | collective-permute-start | bytes 393224 | tf_op jit(solution)/shard_map/ppermute | solution.py:375
  14.6 1.4 %copy-start = (bf16[32,3,8192]{2,0,1:T(8,128)(2,1)S(1)}, bf16[32,3,8192]{2,0,1:T(8,128)(2,1)}, u32[]{:S(2)}) copy-start(bf16[32,3,8192]{2,0,1:T(8,128)(2,1)} %param.4) | copy-start | bytes 4718596
  16.1 1.0 copy-start.2
  17.1 1.0 copy-start.3
  18.1 0.8 copy-start.4
  81.2 18.5 %all-to-all-start.1 = ((bf16[4,32,2048]{2,1,0:T(8,128)(2,1)}), bf16[4,32,2048]{2,1,0:T(8,128)(2,1)S(1)}, u32[]{:S(2)}, u32[]{:S(2)}) async-start(bf16[4,32,2048]{2,1,0:T(8,128)(2,1)} %bitcast.9), calls=%async_computation.1 | async-start | bytes 1048576 | tf_op jit(solution)/shard_map/all_to_all | solution.py:369
  99.7 38.3 %copy-start.1 = (bf16[32,3,8192]{2,0,1:T(8,128)(2,1)S(1)}, bf16[32,3,8192]{2,0,1:T(8,128)(2,1)}, u32[]{:S(2)}) copy-start(bf16[32,3,8192]{2,0,1:T(8,128)(2,1)} %param.4) | copy-start | bytes 4718596
